TPU v7x, 32 devices: a whole 2x2x4 slice. The times are simulated.
32 devices in a mesh: dp: 8 (over z, x), expert: 4 (over y, core).
Axes of the slice: x: 2, y: 2, z: 4, core: 2. Of those that a mesh axis runs over, the one named last changes fastest.
Arguments:
- hidden_in: float32 [12288, 1024], P(('dp', 'expert')), may hold values from -6 to 6
- out_grad: float32 [12288, 1024], P(('dp', 'expert')), may hold values from -6 to 6
- segment_ids: int32 [12288], P(('dp', 'expert')), may hold values from 0 to 415, as said below
- parent_ids: int32 [12288], P(('dp', 'expert')), may hold values from 0 to 413, as said below
- positions: int32 [12288], P(('dp', 'expert')), may hold values from 0 to 190, as said below
- expert_ids: int32 [12288, 8], P(('dp', 'expert')), may hold values from 0 to 31, all different within a row; in each aligned block of 384 rows (0 to 383, 384 to 767, ...) at most 144 rows name the same one
- gate_weights: float32 [12288, 8], P(('dp', 'expert')), may hold values from 0.05 to 0.25
- norm_gains: bfloat16 [2, 1024], replicated, may hold values from 0.5 to 1.5
- qkv_weight: bfloat16 [1024, 2048], replicated, may hold values from -0.1875 to 0.1875
- out_weight: bfloat16 [1024, 1024], replicated, may hold values from -1.5 to 1.5
- gate_up_weight: bfloat16 [32, 1024, 1024], P('expert'), may hold values from -0.1875 to 0.1875
- down_weight: bfloat16 [32, 512, 1024], P('expert'), may hold values from -1 to 1
- gain_moment: float32 [2, 1024], replicated, may hold values from 6144 to 737280
- qkv_rows: float32 [1024], replicated, may hold values from 24576 to 2949120
- qkv_cols: float32 [2048], replicated, may hold values from 3072 to 393216
- out_rows: float32 [1024], replicated, may hold values from 1 to 1000
- out_cols: float32 [1024], replicated, may hold values from 1 to 1000
- gateup_rows: float32 [32, 1024], P('expert'), may hold values from 307 to 36864
- gateup_cols: float32 [32, 1024], P('expert'), may hold values from 1 to 1000
- down_rows: float32 [32, 512], P('expert'), may hold values from 1 to 1000
- down_cols: float32 [32, 1024], P('expert'), may hold values from 1 to 1000
Outputs:
- block_out: float32 [12288, 1024], P(('dp', 'expert'))
- input_grad: float32 [12288, 1024], P(('dp', 'expert'))
- update_rms: float32 [5], replicated
- gains_update: float32 [2, 1024], P(None, 'dp')
- gain_moment_new: float32 [2, 1024], P(None, 'dp')
- qkv_new: float32 [1024, 2048], P('dp')
- qkv_rows_new: float32 [1024], P('dp')
- qkv_cols_new: float32 [2048], replicated
- out_new: float32 [1024, 1024], P('dp')
- out_rows_new: float32 [1024], P('dp')
- out_cols_new: float32 [1024], replicated
- gate_up_new: float32 [32, 1024, 1024], P('expert', 'dp')
- gateup_rows_new: float32 [32, 1024], P('expert', 'dp')
- gateup_cols_new: float32 [32, 1024], P('expert')
- down_new: float32 [32, 512, 1024], P('expert', 'dp')
- down_rows_new: float32 [32, 512], P('expert', 'dp')
- down_cols_new: float32 [32, 1024], P('expert')
Inputs may be any that keep to these rules, and one draw needn't show every extreme that they name: `segment_ids`: each 384 consecutive tokens form one tree: a trunk of 128 tokens, then four regions of 64 tokens, each a branch followed by two leaves, every segment nonempty. Tree t's trunk is segment 13 t, its branch b (0 to 3) is 13 t + 1 + 3 b, that branch's leaves 13 t + 2 + 3 b and 13 t + 3 + 3 b. `parent_ids`: A leaf token's entry is its branch's segment, a branch token's is its trunk's segment, a trunk token's is its own segment. `positions`: A token's distance from its tree's root along its path: trunk tokens 0 to 127 in order, a branch continues from 128, each of its leaves from the end of the branch. `expert_ids`: each row names 8 different experts. In the rows of one device no expert is named by more than 144 rows, a bound that some block reaches in some devices' rows.
All inputs are finite; a program needn't handle non-finite values.
Results may differ from a plain program's by a relative error of at most 0.019.
Values may be sent and summed in bfloat16 or wider, within the bound.
A program may use at most 256 MiB of HBM per device.

v0:
```python
import functools
import math

import jax
import jax.numpy as jnp
from jax import lax
from jax.experimental import pallas as pl
from jax.experimental.pallas import tpu as pltpu
from jax.sharding import PartitionSpec as P

VM = 60 * 1024 * 1024
SCALE = 1e6


def lasts(microseconds):
    return pl.CostEstimate(
        flops=int(microseconds * SCALE), bytes_accessed=1024, transcendentals=0
    )


def dot(a, b, ca=1, cb=0):
    return lax.dot_general(a, b, (((ca,), (cb,)), ((), ())), preferred_element_type=jnp.float32)


def one_hot(code, capacity):
    count, rows = code.shape
    place = lax.broadcasted_iota(jnp.int32, (capacity, rows), 0).astype(jnp.float32)
    return [place == code[j : j + 1, :] for j in range(count)]


def expert_kernel(j, owners, tiles, waits, s_ref, rec_hbm, arr_hbm, scale_ref, up_hbm, down_hbm, *refs):
    (keep_hbm, give_hbm, back_hbm, mix_hbm,
     rec_s, arr_s, up_s, down_s, act_s, gug_s, wg_s, wd_s, parts_s, out_s, in_sem, out_sem) = refs[waits:]
    rows, ff = act_s.shape
    width = up_s.shape[0]
    sources, capacity = rec_s.shape[0], rec_s.shape[1]
    tile = rows // tiles
    per = sources // tiles

    def load(src, dst, at):
        copy = pltpu.make_async_copy(src, dst, in_sem.at[at])
        copy.start()
        return copy

    def load_rows(hbm, held, t, at):
        span = slice(t * per, (t + 1) * per)
        return load(hbm.at[j, span], held.at[span], at)

    expert = s_ref[0] + j
    rec_in = [load_rows(rec_hbm, rec_s, 0, 0)]
    up_in = load(up_hbm.at[expert], up_s, 2 * tiles)
    arr_in = [load_rows(arr_hbm, arr_s, 0, tiles)]
    down_in = load(down_hbm.at[expert], down_s, 2 * tiles + 1)
    for t in range(1, tiles):
        rec_in.append(load_rows(rec_hbm, rec_s, t, t))
        arr_in.append(load_rows(arr_hbm, arr_s, t, tiles + t))
    def products(t):
        span = slice(t * per, (t + 1) * per)
        return (
            dot(rec_s[span].reshape(tile, width), up_s[...]),
            dot(arr_s[span].reshape(tile, width), down_s[...], 1, 1),
        )

    for copy in (up_in, down_in, rec_in[0], arr_in[0]):
        copy.wait()
    following = products(0)
    for t in range(tiles):
        at = slice(t * tile, (t + 1) * tile)
        gate_up, act_grad = following
        if t + 1 < tiles:
            rec_in[t + 1].wait()
            arr_in[t + 1].wait()
            following = products(t + 1)
        gate = gate_up[:, :ff]
        up = gate_up[:, ff:]
        sig = 1.0 / (1.0 + jnp.exp(-gate))
        silu = gate * sig
        act_s[at, :] = (silu * up).astype(jnp.bfloat16)
        gug_s[at, :ff] = (act_grad * up * sig * (1.0 + gate * (1.0 - sig))).astype(jnp.bfloat16)
        gug_s[at, ff:] = (act_grad * silu).astype(jnp.bfloat16)
    wg_s[...] = dot(rec_s[...].reshape(rows, width), gug_s[...], 0, 0)
    wd_s[...] = dot(act_s[...], arr_s[...].reshape(rows, width), 0, 0)
    bit = s_ref[1]
    up_rows = width // owners
    down_rows = ff // owners
    leaving = []
    for k, (hbm, side) in enumerate(((give_hbm, 1 - bit), (keep_hbm, bit))):
        for slot in range(owners // 2):
            owner = 2 * slot + side
            parts_s[k, slot, :up_rows, :] = wg_s[
                pl.ds(pl.multiple_of(owner * up_rows, up_rows), up_rows), :
            ].astype(jnp.bfloat16)
            parts_s[k, slot, up_rows:, :] = wd_s[
                pl.ds(pl.multiple_of(owner * down_rows, down_rows), down_rows), :
            ].astype(jnp.bfloat16)
        copy = pltpu.make_async_copy(parts_s.at[k], hbm, out_sem.at[k])
        copy.start()
        leaving.append(copy)
    for t in range(tiles):
        at = slice(t * tile, (t + 1) * tile)
        out_s[0, at] = dot(gug_s[at, :], up_s[...], 1, 1).astype(jnp.bfloat16)
        scale = scale_ref[0, t * per : (t + 1) * per].reshape(tile, 1)
        out_s[1, at] = (dot(act_s[at, :], down_s[...]) * scale).astype(jnp.bfloat16)
        for k, hbm in enumerate((back_hbm, mix_hbm)):
            copy = pltpu.make_async_copy(out_s.at[k, at], hbm.at[at], out_sem.at[2 + 2 * t + k])
            copy.start()
            leaving.append(copy)
    for copy in leaving:
        copy.wait()


def run_expert(scalars, j, received, arrived, scale, up_w, down_w, owners, after=()):
    count, sources, capacity, width = received.shape
    ff = down_w.shape[1]
    rows = sources * capacity
    tiles = 2
    share = (owners // 2, (width + ff) // owners, width)
    slots = jax.ShapeDtypeStruct((rows, width), jnp.bfloat16)
    parts = jax.ShapeDtypeStruct(share, jnp.bfloat16)
    anywhere = pl.BlockSpec(memory_space=pl.ANY)
    return pl.pallas_call(
        functools.partial(expert_kernel, j, owners, tiles, len(after)),
        out_shape=(parts, parts, slots, slots),
        grid_spec=pltpu.PrefetchScalarGridSpec(
            num_scalar_prefetch=1,
            grid=(1,),
            in_specs=[
                anywhere,
                anywhere,
                pl.BlockSpec((1, sources, capacity, 1), lambda g, s: (j, 0, 0, 0)),
                anywhere,
                anywhere,
            ]
            + [anywhere] * len(after),
            out_specs=[anywhere] * 4,
            scratch_shapes=[
                pltpu.VMEM((sources, capacity, width), jnp.bfloat16),
                pltpu.VMEM((sources, capacity, width), jnp.bfloat16),
                pltpu.VMEM((width, 2 * ff), jnp.bfloat16),
                pltpu.VMEM((ff, width), jnp.bfloat16),
                pltpu.VMEM((rows, ff), jnp.bfloat16),
                pltpu.VMEM((rows, 2 * ff), jnp.bfloat16),
                pltpu.VMEM((width, 2 * ff), jnp.float32),
                pltpu.VMEM((ff, width), jnp.float32),
                pltpu.VMEM((2,) + share, jnp.bfloat16),
                pltpu.VMEM((2, rows, width), jnp.bfloat16),
                pltpu.SemaphoreType.DMA((2 * tiles + 2,)),
                pltpu.SemaphoreType.DMA((2 + 2 * tiles,)),
            ],
        ),
        compiler_params=pltpu.CompilerParams(vmem_limit_bytes=VM),
        cost_estimate=lasts(18),
        name="expert_%d" % j,
    )(scalars, received, arrived, scale, up_w, down_w, *after)


HEADS = 16
KV_HEADS = 8
HEAD_DIM = 64
EPS_NORM = 1e-06
ROPE_BASE = 10000.0
MASKED = -1e30
LANES = 128


def spread(row):
    rows = row.shape[1]
    by_column = jnp.broadcast_to(row.astype(jnp.float32), (rows, rows))
    return by_column, by_column.T


def mask_and_angles(ids_ref):
    seg_k, seg_q = spread(ids_ref[0:1, :])
    par_k, par_q = spread(ids_ref[1:2, :])
    pos_k, pos_q = spread(ids_ref[2:3, :])
    seen = ((seg_k == seg_q) | (seg_k == par_q) | (seg_k == par_k)) & (pos_k <= pos_q)
    bias = jnp.where(seen, 0.0, MASKED)
    lane = lax.broadcasted_iota(jnp.int32, (seg_k.shape[0], LANES), 1)
    half = HEAD_DIM // 2
    place = lax.rem(lane, half).astype(jnp.float32)
    frequency = jnp.exp(place * (-2.0 * math.log(ROPE_BASE) / HEAD_DIM))
    angles = pos_q[:, :LANES] * frequency
    front = lax.rem(lane, HEAD_DIM) < half
    sine = jnp.sin(angles)
    return bias, jnp.cos(angles), jnp.where(front, -sine, sine), front, lane


def turned(block, cosine, sine, front):
    other = jnp.where(
        front,
        pltpu.roll(block, LANES - HEAD_DIM // 2, 1),
        pltpu.roll(block, HEAD_DIM // 2, 1),
    )
    return block * cosine + other * sine


def two_diagonal(pair, which, lane):
    rolled = pltpu.roll(pair, HEAD_DIM, 1)
    first, last = (pair, rolled) if which == 0 else (rolled, pair)
    low = lane < HEAD_DIM
    return jnp.concatenate(
        [jnp.where(low, first, 0.0), jnp.where(low, 0.0, last)], axis=0
    ).astype(jnp.bfloat16)


def column_block(index):
    return pl.ds(pl.multiple_of(index * LANES, LANES), LANES)


def attend_kernel(hidden_ref, ids_ref, gains_ref, qkv_w_hbm, out_w_hbm,
                  normed_hbm, qkv_hbm, attended_hbm, lse_ref, middle_ref, normed_f_ref,
                  normed_ref, qkv_ref, attended_ref, qkv_w_ref, out_w_ref, proj_s, bias_s, sem):
    moving = [
        pltpu.make_async_copy(src, dst, sem.at[i])
        for i, (src, dst) in enumerate(
            (
                (qkv_w_hbm, qkv_w_ref),
                (out_w_hbm, out_w_ref),
                (normed_ref, normed_hbm),
                (qkv_ref, qkv_hbm),
                (attended_ref, attended_hbm),
            )
        )
    ]
    moving[0].start()
    moving[1].start()
    rows = hidden_ref.shape[0]
    att = HEADS * HEAD_DIM
    kv = KV_HEADS * HEAD_DIM
    hidden = hidden_ref[...]
    gains = gains_ref[...].astype(jnp.float32)
    inverse = lax.rsqrt(jnp.mean(hidden * hidden, axis=-1, keepdims=True) + EPS_NORM)
    normed_ref[...] = (hidden * inverse * gains[0:1, :]).astype(jnp.bfloat16)
    moving[2].start()
    bias, cosine, sine, front, lane = mask_and_angles(ids_ref)
    bias_s[...] = bias
    moving[0].wait()
    proj_s[...] = dot(normed_ref[...], qkv_w_ref[...])
    lse_ref[...] = jnp.zeros_like(lse_ref)

    def pair_step(p, carry):
        key_at = column_block(att // LANES + p)
        value_at = column_block((att + kv) // LANES + p)
        keys = turned(proj_s[:, key_at], cosine, sine, front).astype(jnp.bfloat16)
        values = proj_s[:, value_at].astype(jnp.bfloat16)
        qkv_ref[:, key_at] = keys
        qkv_ref[:, value_at] = values
        keys = keys.astype(jnp.float32)
        values = values.astype(jnp.float32)
        for which in range(2):
            query_at = column_block(2 * p + which)
            queries = turned(proj_s[:, query_at], cosine, sine, front).astype(jnp.bfloat16)
            queries = (queries.astype(jnp.float32) * HEAD_DIM**-0.5).astype(jnp.bfloat16)
            qkv_ref[:, query_at] = queries
            scores = dot(queries, two_diagonal(keys, which, lane), 1, 1)
            probs = []
            for head in range(2):
                part = scores[:, head * rows : (head + 1) * rows] + bias_s[...]
                top = jnp.max(part, axis=-1, keepdims=True)
                part = jnp.exp(part - top)
                total = jnp.sum(part, axis=-1, keepdims=True)
                probs.append((part * (1.0 / total)).astype(jnp.bfloat16))
                at = 4 * p + 2 * which + head
                lse_ref[...] = jnp.where(lane == at, top + jnp.log(total), lse_ref[...])
            attended_ref[:, query_at] = dot(
                jnp.concatenate(probs, axis=1), two_diagonal(values, which, lane)
            ).astype(jnp.bfloat16)
        return carry

    lax.fori_loop(0, KV_HEADS // 2, pair_step, 0)
    moving[3].start()
    moving[4].start()
    moving[1].wait()
    middle = hidden + dot(attended_ref[...], out_w_ref[...])
    middle_ref[...] = middle
    inverse_f = lax.rsqrt(jnp.mean(middle * middle, axis=-1, keepdims=True) + EPS_NORM)
    normed_f_ref[...] = (middle * inverse_f * gains[1:2, :]).astype(jnp.bfloat16)
    for copy in moving[2:]:
        copy.wait()


def attend(hidden, ids, gains, qkv_w, out_w):
    rows, width = hidden.shape
    shape = jax.ShapeDtypeStruct
    return pl.pallas_call(
        attend_kernel,
        out_shape=(
            shape((rows, width), jnp.bfloat16),
            shape((rows, qkv_w.shape[1]), jnp.bfloat16),
            shape((rows, out_w.shape[0]), jnp.bfloat16),
            shape((rows, LANES), jnp.float32),
            shape((rows, width), jnp.float32),
            shape((rows, width), jnp.bfloat16),
        ),
        in_specs=[pl.BlockSpec(memory_space=pltpu.VMEM)] * 3 + [pl.BlockSpec(memory_space=pl.ANY)] * 2,
        out_specs=[pl.BlockSpec(memory_space=pl.ANY)] * 3 + [pl.BlockSpec(memory_space=pltpu.VMEM)] * 3,
        scratch_shapes=[
            pltpu.VMEM((rows, width), jnp.bfloat16),
            pltpu.VMEM((rows, qkv_w.shape[1]), jnp.bfloat16),
            pltpu.VMEM((rows, out_w.shape[0]), jnp.bfloat16),
            pltpu.VMEM(qkv_w.shape, jnp.bfloat16),
            pltpu.VMEM(out_w.shape, jnp.bfloat16),
            pltpu.VMEM((rows, qkv_w.shape[1]), jnp.float32),
            pltpu.VMEM((rows, rows), jnp.float32),
            pltpu.SemaphoreType.DMA((5,)),
        ],
        compiler_params=pltpu.CompilerParams(vmem_limit_bytes=VM),
        cost_estimate=lasts(18),
        name="attend",
    )(hidden, ids, gains, qkv_w, out_w)


def attend_back_kernel(waits, grad_ref, middle_ref, normed_grad_ref, lse_ref, ids_ref, gains_ref,
                       hidden_hbm, normed_hbm, qkv_hbm, attended_hbm, qkv_w_hbm, out_w_hbm, *refs):
    (input_grad_ref, dense_hbm, dense_ref, hidden_ref, normed_ref, qkv_ref, attended_ref, qkv_w_ref, out_w_ref,
     proj_s, bias_s, back_s, sem) = refs[waits:]
    rows, width = hidden_ref.shape
    incoming = {
        name: pltpu.make_async_copy(src, dst, sem.at[i])
        for i, (name, src, dst) in enumerate(
            (
                ("attended", attended_hbm, attended_ref),
                ("out_w", out_w_hbm, out_w_ref),
                ("qkv", qkv_hbm, qkv_ref),
                ("normed", normed_hbm, normed_ref),
                ("qkv_w", qkv_w_hbm, qkv_w_ref),
                ("hidden", hidden_hbm, hidden_ref),
            )
        )
    }
    for copy in incoming.values():
        copy.start()
    leaving = []

    def leave(span):
        copy = pltpu.make_async_copy(dense_ref.at[:, span], dense_hbm.at[:, span], sem.at[6 + len(leaving)])
        copy.start()
        leaving.append(copy)

    att = HEADS * HEAD_DIM
    kv = KV_HEADS * HEAD_DIM
    gains = gains_ref[...].astype(jnp.float32)
    normed_grad = normed_grad_ref[...]
    middle = middle_ref[...]
    inverse_f = lax.rsqrt(jnp.mean(middle * middle, axis=-1, keepdims=True) + EPS_NORM)
    gain_f = jnp.sum(normed_grad * middle * inverse_f, axis=0, keepdims=True)
    weighted = normed_grad * gains[1:2, :]
    middle_grad = grad_ref[...] + (
        inverse_f * weighted
        - middle * (inverse_f * inverse_f * inverse_f)
        * jnp.mean(weighted * middle, axis=-1, keepdims=True)
    )
    input_grad_ref[...] = middle_grad
    branch = middle_grad.astype(jnp.bfloat16)
    columns = att + 2 * kv
    incoming["attended"].wait()
    dense_ref[:, columns : columns + width] = dot(attended_ref[...], branch, 0, 0).astype(jnp.bfloat16)
    leave(slice(columns, columns + width))
    incoming["out_w"].wait()
    back_s[...] = dot(branch, out_w_ref[...], 1, 1).astype(jnp.bfloat16)
    bias, cosine, sine, front, lane = mask_and_angles(ids_ref)
    bias_s[...] = bias
    low = lane < HEAD_DIM
    incoming["qkv"].wait()

    def pair_step(p, carry):
        key_at = column_block(att // LANES + p)
        value_at = column_block((att + kv) // LANES + p)
        keys = qkv_ref[:, key_at].astype(jnp.float32)
        values = qkv_ref[:, value_at].astype(jnp.float32)
        key_grads = []
        value_grads = []
        for which in range(2):
            query_at = column_block(2 * p + which)
            queries = qkv_ref[:, query_at]
            back = back_s[:, query_at]
            key_two = two_diagonal(keys, which, lane)
            scores = dot(queries, key_two, 1, 1)
            prob_grads = dot(back, two_diagonal(values, which, lane), 1, 1)
            probs = []
            score_grads = []
            for head in range(2):
                at = 4 * p + 2 * which + head
                level = jnp.sum(jnp.where(lane == at, lse_ref[...], 0.0), axis=-1, keepdims=True)
                span = slice(head * rows, (head + 1) * rows)
                prob = jnp.exp(scores[:, span] + bias_s[...] - level)
                prob_grad = prob_grads[:, span]
                row_dot = jnp.sum(prob * prob_grad, axis=-1, keepdims=True)
                probs.append(prob.astype(jnp.bfloat16))
                score_grads.append((prob * (prob_grad - row_dot)).astype(jnp.bfloat16))
            score_grads = jnp.concatenate(score_grads, axis=1)
            query_grad = dot(score_grads, key_two) * HEAD_DIM**-0.5
            proj_s[:, query_at] = turned(query_grad, cosine, -sine, front).astype(jnp.bfloat16)
            for grads, left, right in (
                (key_grads, score_grads, queries),
                (value_grads, jnp.concatenate(probs, axis=1), back),
            ):
                both = dot(left, right, 0, 0)
                first, last = both[:rows], both[rows:]
                if which == 0:
                    grads.append(first + pltpu.roll(last, HEAD_DIM, 1))
                else:
                    grads.append(pltpu.roll(first, HEAD_DIM, 1) + last)
        key_grad = jnp.where(low, key_grads[0], key_grads[1])
        proj_s[:, key_at] = turned(key_grad, cosine, -sine, front).astype(jnp.bfloat16)
        proj_s[:, value_at] = jnp.where(low, value_grads[0], value_grads[1]).astype(jnp.bfloat16)
        return carry

    lax.fori_loop(0, KV_HEADS // 2, pair_step, 0)
    for name in ("normed", "qkv_w", "hidden"):
        incoming[name].wait()
    for first in range(0, columns, columns // 2):
        span = slice(first, first + columns // 2)
        dense_ref[:, span] = dot(normed_ref[...], proj_s[:, span], 0, 0).astype(jnp.bfloat16)
        leave(span)
    normed_grad = dot(proj_s[...], qkv_w_ref[...], 1, 1)
    hidden = hidden_ref[...]
    inverse = lax.rsqrt(jnp.mean(hidden * hidden, axis=-1, keepdims=True) + EPS_NORM)
    gain_a = jnp.sum(normed_grad * hidden * inverse, axis=0, keepdims=True)
    weighted = normed_grad * gains[0:1, :]
    input_grad_ref[...] += inverse * weighted - hidden * (inverse * inverse * inverse) * jnp.mean(
        weighted * hidden, axis=-1, keepdims=True
    )
    both = jnp.concatenate([gain_a, gain_f, jnp.zeros((LANES - 2, width), jnp.float32)], axis=0)
    dense_ref[:, columns + width :] = both.T.astype(jnp.bfloat16)
    leave(slice(columns + width, columns + width + LANES))
    for copy in leaving:
        copy.wait()


def attend_back(hidden, out_grad, middle, normed_f_grad, normed, qkv, attended, lse, ids, gains, qkv_w, out_w, after=()):
    rows, width = hidden.shape
    columns = qkv_w.shape[1] + width + LANES
    return pl.pallas_call(
        functools.partial(attend_back_kernel, len(after)),
        out_shape=(
            jax.ShapeDtypeStruct((rows, width), jnp.float32),
            jax.ShapeDtypeStruct((width, columns), jnp.bfloat16),
        ),
        in_specs=[pl.BlockSpec(memory_space=pltpu.VMEM)] * 6
        + [pl.BlockSpec(memory_space=pl.ANY)] * (6 + len(after)),
        out_specs=[pl.BlockSpec(memory_space=pltpu.VMEM), pl.BlockSpec(memory_space=pl.ANY)],
        scratch_shapes=[
            pltpu.VMEM((width, columns), jnp.bfloat16),
            pltpu.VMEM((rows, width), jnp.float32),
            pltpu.VMEM((rows, width), jnp.bfloat16),
            pltpu.VMEM((rows, qkv_w.shape[1]), jnp.bfloat16),
            pltpu.VMEM((rows, out_w.shape[0]), jnp.bfloat16),
            pltpu.VMEM(qkv_w.shape, jnp.bfloat16),
            pltpu.VMEM(out_w.shape, jnp.bfloat16),
            pltpu.VMEM((rows, qkv_w.shape[1]), jnp.bfloat16),
            pltpu.VMEM((rows, rows), jnp.float32),
            pltpu.VMEM((rows, out_w.shape[0]), jnp.bfloat16),
            pltpu.SemaphoreType.DMA((10,)),
        ],
        compiler_params=pltpu.CompilerParams(vmem_limit_bytes=VM),
        cost_estimate=lasts(26),
        name="attend_back",
    )(out_grad, middle, normed_f_grad, lse, ids, gains, hidden, normed, qkv, attended, qkv_w, out_w, *after)


MESH = pl.DeviceIdType.MESH


def greet(peers):
    barrier = pltpu.get_barrier_semaphore()
    for peer in peers:
        pl.semaphore_signal(barrier, inc=1, device_id=peer, device_id_type=MESH)
    pl.semaphore_wait(barrier, len(peers))


def total_kernel(axis, count, mine_ref, *refs):
    out_ref, got_ref, send_sem, recv_sem = refs[-4:]
    me = lax.axis_index(axis)
    after = [lax.rem(me + k, count) for k in range(count)]
    greet([{axis: after[k]} for k in range(1, count)])
    scatter = [
        pltpu.make_async_remote_copy(
            src_ref=mine_ref.at[after[k]],
            dst_ref=got_ref.at[k],
            send_sem=send_sem.at[0, k],
            recv_sem=recv_sem.at[0, k],
            device_id={axis: after[k]},
            device_id_type=MESH,
        )
        for k in range(1, count)
    ]
    for copy in scatter:
        copy.start()
    total = mine_ref[me]
    for k in range(1, count):
        scatter[k - 1].wait_recv()
        total = total + got_ref[k]
    out_ref[me] = total
    share = [
        pltpu.make_async_remote_copy(
            src_ref=out_ref.at[me],
            dst_ref=out_ref.at[me],
            send_sem=send_sem.at[1, k],
            recv_sem=recv_sem.at[1, k],
            device_id={axis: after[k]},
            device_id_type=MESH,
        )
        for k in range(1, count)
    ]
    for copy in share:
        copy.start()
    for copy in share:
        copy.wait_recv()
    for copy in scatter + share:
        copy.wait_send()


def total_over(values, axis, label, after=()):
    count = lax.axis_size(axis)
    rows = -(-values.shape[0] // (8 * 128 * count)) * 8
    padded = jnp.pad(values, (0, count * rows * 128 - values.shape[0])).reshape(count, rows, 128)
    out = pl.pallas_call(
        functools.partial(total_kernel, axis, count),
        out_shape=jax.ShapeDtypeStruct(padded.shape, jnp.float32),
        in_specs=[pl.BlockSpec(memory_space=pltpu.VMEM)] + [pl.BlockSpec(memory_space=pl.ANY)] * len(after),
        out_specs=pl.BlockSpec(memory_space=pltpu.VMEM),
        scratch_shapes=[
            pltpu.VMEM(padded.shape, jnp.float32),
            pltpu.SemaphoreType.DMA((2, count)),
            pltpu.SemaphoreType.DMA((2, count)),
        ],
        compiler_params=pltpu.CompilerParams(
            collective_id=label, has_side_effects=True, vmem_limit_bytes=16 * 1024 * 1024
        ),
        cost_estimate=lasts(12),
        name="total_%d" % label,
    )(padded, *after)
    return out.reshape(-1)[: values.shape[0]]


def collect_kernel(axis, count, mine_ref, out_ref, send_sem, recv_sem, local_sem):
    me = lax.axis_index(axis)
    after = [lax.rem(me + k, count) for k in range(count)]
    greet([{axis: after[k]} for k in range(1, count)])
    copies = [
        pltpu.make_async_remote_copy(
            src_ref=mine_ref,
            dst_ref=out_ref.at[me],
            send_sem=send_sem.at[k],
            recv_sem=recv_sem.at[k],
            device_id={axis: after[k]},
            device_id_type=MESH,
        )
        for k in range(1, count)
    ]
    for copy in copies:
        copy.start()
    out_ref[me] = mine_ref[...]
    for copy in copies:
        copy.wait()


def collect(values, axis, label):
    count = lax.axis_size(axis)
    return pl.pallas_call(
        functools.partial(collect_kernel, axis, count),
        out_shape=jax.ShapeDtypeStruct((count,) + values.shape, jnp.float32),
        in_specs=[pl.BlockSpec(memory_space=pltpu.VMEM)],
        out_specs=pl.BlockSpec(memory_space=pltpu.VMEM),
        scratch_shapes=[
            pltpu.SemaphoreType.DMA((count,)),
            pltpu.SemaphoreType.DMA((count,)),
            pltpu.SemaphoreType.DMA,
        ],
        compiler_params=pltpu.CompilerParams(
            collective_id=label, has_side_effects=True, vmem_limit_bytes=16 * 1024 * 1024
        ),
        cost_estimate=lasts(4),
        name="collect_%d" % label,
    )(values)


def flipped(axis, mask):
    index = lax.axis_index(axis)
    bit = lax.rem(index // mask, 2)
    return bit, {axis: index + mask - 2 * mask * bit}


PAIR = 2
ROUTE_ROWS = 32


class Pusher:
    def __init__(self, send_sem, recv_sem):
        self.send_sem, self.recv_sem, self.copies = send_sem, recv_sem, []

    def __call__(self, src, dst, peer):
        at = len(self.copies)
        copy = pltpu.make_async_remote_copy(
            src_ref=src,
            dst_ref=dst,
            send_sem=self.send_sem.at[at],
            recv_sem=self.recv_sem.at[at],
            device_id=peer,
            device_id_type=MESH,
        )
        copy.start()
        self.copies.append(copy)
        return copy

    def finish(self):
        for copy in self.copies:
            copy.wait_send()


def picked(code, capacity):
    return jnp.concatenate(
        [c.astype(jnp.float32) for c in one_hot(code, capacity)], axis=0
    ).astype(jnp.bfloat16)


def gather_kernel(capacity, experts_here, half_experts, top, token_ref, grad_ref, chip_grad_ref, pair_grad_ref,
                  rec_ref, arr_ref, scale_ref, code_ref, tokens, grads, weight_s, stage, send_sem, recv_sem, local_sem):
    rows = token_ref.shape[0]
    half = rows // 2
    first = lax.axis_index("expert") * experts_here + lax.rem(lax.axis_index("dp") // PAIR, 2) * half_experts
    _, core = flipped("expert", 1)
    _, chip = flipped("expert", 2)
    _, pair = flipped("dp", PAIR)
    greet([core, chip, pair])
    push = Pusher(send_sem, recv_sem)
    everything, routing = slice(None), slice(rows, rows + ROUTE_ROWS)
    to_chip = push(token_ref, tokens.at[2], chip)
    to_pair = push(token_ref, tokens.at[4], pair)
    route_both = push(pair_grad_ref.at[routing], grads.at[6, routing], chip)
    to_core = push(token_ref, tokens.at[1], core)
    grad_core = push(grad_ref, grads.at[1], core)
    grad_chip_core = push(chip_grad_ref, grads.at[3], core)
    grad_pair_core = push(pair_grad_ref, grads.at[5], core)

    earlier = lax.broadcasted_iota(jnp.int32, (rows, rows), 0)
    later = lax.broadcasted_iota(jnp.int32, (rows, rows), 1)
    before = jnp.where(earlier < later, 1.0, 0.0).astype(jnp.bfloat16)

    def route(r, table):
        table = table.astype(jnp.float32)
        ids = table[:top]
        gates = table[top : 2 * top] + table[2 * top : 3 * top]
        hits = [ids == (first + j).astype(jnp.float32) for j in range(half_experts)]
        named = jnp.concatenate(
            [jnp.max(jnp.where(hit, 1.0, 0.0), axis=0, keepdims=True) for hit in hits], axis=0
        )
        weight_s[r] = jnp.concatenate(
            [jnp.sum(jnp.where(hit, gates, 0.0), axis=0, keepdims=True) for hit in hits], axis=0
        )
        code_ref[r] = jnp.where(named > 0.0, dot(named.astype(jnp.bfloat16), before), -1.0)

    leaving = []

    def select(r, source, out_ref, weighted):
        slot = len(leaving) % stage.shape[0]
        if len(leaving) >= stage.shape[0]:
            leaving[len(leaving) - stage.shape[0]].wait()
        chosen = one_hot(code_ref[r], capacity)
        pick = jnp.concatenate([c.astype(jnp.float32) for c in chosen], axis=0).astype(jnp.bfloat16)
        made = dot(pick, source)
        for j in range(half_experts):
            part = made[j * capacity : (j + 1) * capacity]
            if weighted:
                scale = jnp.sum(
                    jnp.where(chosen[j], weight_s[r, j : j + 1, :], 0.0), axis=1, keepdims=True
                )
                scale_ref[j, r] = scale
                part = part * scale
            stage[slot, j] = part.astype(jnp.bfloat16)
        copy = pltpu.make_async_copy(stage.at[slot], out_ref.at[:, r], local_sem.at[slot])
        copy.start()
        leaving.append(copy)

    def select_grad(r, ref):
        route(r, ref[rows:, :rows])
        select(r, ref[:rows, :], arr_ref, True)

    select_grad(0, grad_ref)
    select(0, token_ref[...], rec_ref, False)
    select_grad(2, chip_grad_ref)
    select_grad(4, pair_grad_ref)
    for r, copy in ((1, grad_core), (3, grad_chip_core), (5, grad_pair_core)):
        copy.wait_recv()
        select_grad(r, grads.at[r])
    to_core.wait_recv()
    select(1, tokens[1], rec_ref, False)
    route_both.wait_recv()
    route_core = push(grads.at[6, routing], grads.at[7, routing], core)
    to_chip.wait_recv()
    both_low = push(tokens.at[2, half:rows], tokens.at[6, half:rows], pair)
    chip_core = push(tokens.at[2], tokens.at[3], core)
    to_pair.wait_recv()
    both_high = push(tokens.at[4, 0:half], tokens.at[6, 0:half], chip)
    pair_core = push(tokens.at[4], tokens.at[5], core)
    grad_low = push(chip_grad_ref.at[half:rows], grads.at[6, half:rows], pair)
    grad_high = push(pair_grad_ref.at[0:half], grads.at[6, 0:half], chip)
    select(2, tokens[2], rec_ref, False)
    select(4, tokens[4], rec_ref, False)
    route(6, grads[6, rows:, :rows])
    route_core.wait_recv()
    route(7, grads[7, rows:, :rows])
    chip_core.wait_recv()
    select(3, tokens[3], rec_ref, False)
    pair_core.wait_recv()
    select(5, tokens[5], rec_ref, False)
    both_low.wait_recv()
    both_high.wait_recv()
    both_core = push(tokens.at[6], tokens.at[7], core)
    select(6, tokens[6], rec_ref, False)
    both_core.wait_recv()
    select(7, tokens[7], rec_ref, False)
    grad_low.wait_recv()
    grad_high.wait_recv()
    grad_both_core = push(grads.at[6, 0:rows], grads.at[7, 0:rows], core)
    select(6, grads[6, :rows], arr_ref, True)
    grad_both_core.wait_recv()
    select(7, grads[7, :rows], arr_ref, True)
    for copy in leaving[-stage.shape[0] :]:
        copy.wait()
    push.finish()


def gather_and_select(token, grad, chip_grad, pair_grad, capacity, experts_here, half_experts, top, label):
    rows, width = token.shape
    vmem = pl.BlockSpec(memory_space=pltpu.VMEM)
    anywhere = pl.BlockSpec(memory_space=pl.ANY)
    slots = jax.ShapeDtypeStruct((half_experts, 8, capacity, width), jnp.bfloat16)
    return pl.pallas_call(
        functools.partial(gather_kernel, capacity, experts_here, half_experts, top),
        out_shape=(
            slots,
            slots,
            jax.ShapeDtypeStruct((half_experts, 8, capacity, 1), jnp.float32),
            jax.ShapeDtypeStruct((8, half_experts, rows), jnp.float32),
        ),
        in_specs=[vmem] * 4,
        out_specs=[anywhere, anywhere, vmem, vmem],
        scratch_shapes=[
            pltpu.VMEM((8, rows, width), jnp.bfloat16),
            pltpu.VMEM((8, rows + ROUTE_ROWS, width), jnp.bfloat16),
            pltpu.VMEM((8, half_experts, rows), jnp.float32),
            pltpu.VMEM((4, half_experts, capacity, width), jnp.bfloat16),
            pltpu.SemaphoreType.DMA((18,)),
            pltpu.SemaphoreType.DMA((18,)),
            pltpu.SemaphoreType.DMA((4,)),
        ],
        compiler_params=pltpu.CompilerParams(
            collective_id=label, has_side_effects=True, vmem_limit_bytes=VM
        ),
        cost_estimate=lasts(44),
        name="gather_and_select",
    )(token, grad, chip_grad, pair_grad)


def fetcher(order, fetched, local_sem, capacity, code_ref):
    depth = fetched.shape[0]
    fetching = []
    done = []

    def fetch():
        n = len(fetching)
        if n < len(order):
            slots, r = order[n]
            fetching.append(
                [
                    pltpu.make_async_copy(
                        ref.at[r * capacity : (r + 1) * capacity],
                        fetched.at[n % depth, j * capacity : (j + 1) * capacity],
                        local_sem.at[n % depth, j],
                    )
                    for j, ref in enumerate(slots)
                ]
            )
            for copy in fetching[-1]:
                copy.start()

    for _ in range(depth - 1):
        fetch()

    def next_sum():
        fetch()
        n = len(done)
        for copy in fetching[n]:
            copy.wait()
        done.append(n)
        return dot(picked(code_ref[order[n][1]], capacity), fetched[n % depth], 0, 0)

    return next_sum


def combine_kernel(capacity, count, code_ref, *refs):
    slots = refs[:count]
    mine_ref, theirs_ref, fetched, local_sem = refs[-4:]
    order = [(slots, r) for r in (7, 6, 3, 2, 5, 4, 1, 0)]
    next_sum = fetcher(order, fetched, local_sem, capacity, code_ref)
    for _, r in order:
        (theirs_ref if r % 2 else mine_ref)[r // 2] = next_sum().astype(jnp.bfloat16)


def combine(code, slots, capacity, after):
    _, count, rows = code.shape
    width = slots[0].shape[1]
    vmem = pl.BlockSpec(memory_space=pltpu.VMEM)
    anywhere = pl.BlockSpec(memory_space=pl.ANY)
    four = jax.ShapeDtypeStruct((4, rows, width), jnp.bfloat16)
    return pl.pallas_call(
        functools.partial(combine_kernel, capacity, count),
        out_shape=(four, four),
        in_specs=[vmem] + [anywhere] * (count + len(after)),
        out_specs=[vmem, vmem],
        scratch_shapes=[
            pltpu.VMEM((4, count * capacity, width), jnp.bfloat16),
            pltpu.SemaphoreType.DMA((4, count)),
        ],
        compiler_params=pltpu.CompilerParams(vmem_limit_bytes=VM),
        cost_estimate=lasts(12),
        name="combine",
    )(code, *slots, *after)


def return_kernel(capacity, count, far_mask, code_ref, mine_ref, theirs_ref, go_ref, *refs):
    mixes = refs[:count]
    (out_ref, near_ref, far_ref, come_ref, fetched, core_got, own, theirs_mix, core_got_mix, half_pair, half_chip, from_chip,
     from_pair, send_sem, recv_sem, local_sem) = refs[-16:]
    rows = out_ref.shape[0]
    half = rows // 2
    _, core = flipped("expert", 1)
    _, chip = flipped("expert", 2)
    _, pair = flipped("dp", PAIR)
    _, far = flipped("dp", far_mask)
    greet([core, chip, pair, far])
    push = Pusher(send_sem, recv_sem)
    beside = push(go_ref, come_ref, far)
    crossing = {i: push(theirs_ref.at[i], core_got.at[i], core) for i in (3, 1, 2, 0)}
    order = [(mixes, r) for r in (7, 6, 3, 2, 5, 4, 1, 0)]
    next_sum = fetcher(order, fetched, local_sem, capacity, code_ref)

    def plus(a, b):
        return (a.astype(jnp.float32) + b.astype(jnp.float32)).astype(jnp.bfloat16)

    def mix(i, ref, at):
        theirs_mix[i] = next_sum().astype(jnp.bfloat16)
        copy = push(theirs_mix.at[i], core_got_mix.at[i], core)
        mine = next_sum()
        copy.wait_recv()
        ref[at] = plus(mine, core_got_mix[i])

    crossing[3].wait_recv()
    own[3] = plus(mine_ref[3], core_got[3])
    at_pair = push(own.at[3, 0:half], half_pair, pair)
    at_chip = push(own.at[3, half:rows], half_chip, chip)
    crossing[1].wait_recv()
    own[1] = plus(mine_ref[1], core_got[1])
    low_chip = push(own.at[1, half:rows], from_chip.at[half:rows], chip)
    crossing[2].wait_recv()
    own[2] = plus(mine_ref[2], core_got[2])
    high_pair = push(own.at[2, 0:half], from_pair.at[0:half], pair)
    crossing[0].wait_recv()
    out_ref[...] = mine_ref[0].astype(jnp.float32) + core_got[0].astype(jnp.float32)
    mix(3, far_ref, 1)
    mix(1, far_ref, 0)
    at_pair.wait_recv()
    own[1, :half] = plus(own[1, :half], half_pair[...])
    high_chip = push(own.at[1, 0:half], from_chip.at[0:half], chip)
    at_chip.wait_recv()
    own[2, half:] = plus(own[2, half:], half_chip[...])
    low_pair = push(own.at[2, half:rows], from_pair.at[half:rows], pair)
    mix(2, near_ref, 1)
    mix(0, near_ref, 0)
    low_chip.wait_recv()
    high_pair.wait_recv()
    high_chip.wait_recv()
    low_pair.wait_recv()
    out_ref[...] += from_chip[...].astype(jnp.float32) + from_pair[...].astype(jnp.float32)
    beside.wait_recv()
    push.finish()


def return_sums(code, mine, theirs, mixes, capacity, go, far_mask, label, after):
    _, count, rows = code.shape
    width = mine.shape[2]
    vmem = pl.BlockSpec(memory_space=pltpu.VMEM)
    anywhere = pl.BlockSpec(memory_space=pl.ANY)
    four = pltpu.VMEM((4, rows, width), jnp.bfloat16)
    two = jax.ShapeDtypeStruct((2, rows, width), jnp.bfloat16)
    return pl.pallas_call(
        functools.partial(return_kernel, capacity, count, far_mask),
        out_shape=(
            jax.ShapeDtypeStruct((rows, width), jnp.float32),
            two,
            two,
            jax.ShapeDtypeStruct(go.shape, jnp.bfloat16),
        ),
        in_specs=[vmem] * 3 + [anywhere] * (1 + count + len(after)),
        out_specs=[vmem] * 3 + [anywhere],
        scratch_shapes=[pltpu.VMEM((4, count * capacity, width), jnp.bfloat16), four, four, four, four]
        + [pltpu.VMEM((rows // 2, width), jnp.bfloat16)] * 2
        + [pltpu.VMEM((rows, width), jnp.bfloat16)] * 2
        + [
            pltpu.SemaphoreType.DMA((15,)),
            pltpu.SemaphoreType.DMA((15,)),
            pltpu.SemaphoreType.DMA((4, count)),
        ],
        compiler_params=pltpu.CompilerParams(
            collective_id=label, has_side_effects=True, vmem_limit_bytes=VM
        ),
        cost_estimate=lasts(37),
        name="return_sums",
    )(code, mine, theirs, go, *mixes, *after)


def settle_kernel(waits, bit_ref, keep_hbm, got_hbm, *refs):
    stay_ref, go_ref = refs[waits : waits + 2]
    keep_ref, got_ref, sem = refs[-3:]
    arriving = [
        pltpu.make_async_copy(src, dst, sem.at[i])
        for i, (src, dst) in enumerate(((keep_hbm, keep_ref), (got_hbm, got_ref)))
    ]
    for copy in arriving:
        copy.start()
    for copy in arriving:
        copy.wait()
    bit = bit_ref[0]
    for high in range(keep_ref.shape[0]):
        for low in range(keep_ref.shape[2]):
            for ref, side in ((stay_ref, bit), (go_ref, 1 - bit)):
                total = keep_ref[high, side, low].astype(jnp.float32) + got_ref[
                    high, side, low
                ].astype(jnp.float32)
                ref[high, low] = total.astype(jnp.bfloat16)


def settle(keep, got, mask, label, after, passed=()):
    count, rows, columns = keep.shape
    low = 1 if mask == PAIR else 2
    shape = (count // 2 // low, 2, low, rows, columns)
    half = jax.ShapeDtypeStruct((count // 2 // low, low, rows, columns), jnp.bfloat16)
    bit = lax.rem(lax.axis_index("dp") // mask, 2)
    vmem = pl.BlockSpec(memory_space=pltpu.VMEM)
    anywhere = pl.BlockSpec(memory_space=pl.ANY)
    stay, go, *passed = pl.pallas_call(
        functools.partial(settle_kernel, len(after) + len(passed)),
        out_shape=[half, half] + [jax.ShapeDtypeStruct(p.shape, p.dtype) for p in passed],
        in_specs=[pl.BlockSpec(memory_space=pltpu.SMEM)] + [anywhere] * (2 + len(after) + len(passed)),
        scratch_shapes=[
            pltpu.VMEM(shape, jnp.bfloat16),
            pltpu.VMEM(shape, jnp.bfloat16),
            pltpu.SemaphoreType.DMA((2,)),
        ],
        out_specs=[vmem, vmem] + [anywhere] * len(passed),
        input_output_aliases={3 + len(after) + i: 2 + i for i in range(len(passed))},
        compiler_params=pltpu.CompilerParams(vmem_limit_bytes=VM),
        cost_estimate=lasts(3),
        name="settle_%s" % label,
    )(bit.reshape(1), keep.reshape(shape), got.reshape(shape), *after, *passed)
    return stay.reshape(-1, rows, columns), go.reshape(-1, rows, columns), *passed


def settle_mix_kernel(near_ref, got_ref, *refs):
    refs[-1][...] = (near_ref[1].astype(jnp.float32) + got_ref[1].astype(jnp.float32)).astype(jnp.bfloat16)


def settle_mix(near, got, after):
    vmem = pl.BlockSpec(memory_space=pltpu.VMEM)
    return pl.pallas_call(
        settle_mix_kernel,
        out_shape=jax.ShapeDtypeStruct(near.shape[1:], jnp.bfloat16),
        in_specs=[vmem] * 2 + [pl.BlockSpec(memory_space=pl.ANY)] * len(after),
        out_specs=vmem,
        compiler_params=pltpu.CompilerParams(vmem_limit_bytes=VM),
        cost_estimate=lasts(3),
        name="settle_mix",
    )(near, got, *after)


EPS_STAT = 1e-30
STAT_DECAY = 0.5
LEARN_RATE = 0.5
CLIP_LEVEL = 0.05


def decayed(old, new):
    return STAT_DECAY * old + (1.0 - STAT_DECAY) * new


def finish_kernel(count, groups, half, orders, spans, *refs):
    bits = count.bit_length() - 1
    steps = len(orders[0])
    (mine_hbm, own_0, own_1, got_0, got_1, stay_2, come_2, keep_3, come_3, near_mix_ref, got_mix_ref,
     up_rows_ref, down_rows_ref, up_cols_ref, down_cols_ref, qkv_rows_ref, out_rows_ref, moments_ref, qkv_cols_ref,
     out_cols_ref) = refs[:20]
    (dense_ref, ends_ref, pair_mix_ref, out_ref, sums_ref, up_new_ref, down_new_ref, dense_out_ref,
     dense_new_ref) = refs[20:29]
    sum_ref, first_got, *got = refs[29 : 31 + steps]
    (mine_ref, load_sem, go_s, far_go_s, far_stay_s, far_got_s, mix_s, pay_s, got_s, dense_pay_s, dense_got_s, spread_s,
     up_old_ref, down_old_ref, dense_old_ref, dense_cols_ref, send_sem, recv_sem) = refs[31 + steps :]
    width = up_rows_ref.shape[1]
    ff = down_rows_ref.shape[1]
    wide = width // 2
    own_up = width // count
    own_down = ff // count
    me = lax.axis_index("dp")
    place = lax.axis_index("expert")
    after = [lax.rem(me + k, count) for k in range(count)]
    beside = [lax.rem(place + k, groups) for k in range(groups)]
    pair_bit, pair = flipped("dp", PAIR)
    far_bit, far = flipped("dp", FAR)
    core, core_peer = flipped("expert", 1)
    chip, chip_peer = flipped("expert", 2)
    links = [flipped("dp", 1 << b) for b in range(bits)] + [(chip, chip_peer)]
    whole = (slice(None),) * bits
    loading = pltpu.make_async_copy(mine_hbm.at[whole + (core,)], mine_ref, load_sem)
    loading.start()
    greet([{"dp": after[k]} for k in range(1, count)] + [{"expert": beside[k]} for k in range(1, groups)])
    push = Pusher(send_sem, recv_sem)

    def plus(a, b):
        return (a.astype(jnp.float32) + b.astype(jnp.float32)).astype(jnp.bfloat16)

    flying = [
        push(mine_hbm.at[whole + (1 - core, slice(None), slice(None), span)], first_got.at[..., span], core_peer)
        for span in spans
    ]
    for low in range(2):
        far_go_s[low] = plus(keep_3[1 - far_bit, low], come_3[1 - far_bit, low])
    far_exchange = push(far_go_s, far_got_s, far)
    go_s[0] = plus(stay_2[1 - pair_bit], come_2[1 - pair_bit])
    cross_2 = push(go_s.at[0], ends_ref.at[2], pair)
    mix_s[...] = plus(near_mix_ref[1], got_mix_ref[1])
    cross_mix = push(mix_s, pair_mix_ref, pair)
    ends_ref[0] = plus(stay_2[pair_bit], come_2[pair_bit])
    for low in range(2):
        far_stay_s[low] = plus(keep_3[far_bit, low], come_3[far_bit, low])

    def own_columns(*tables):
        here = pl.ds(pl.multiple_of(me * LANES, LANES), LANES)
        rows = [table[:, here] for table in tables]
        return padded(jnp.concatenate(rows, axis=0)).T

    def padded(rows):
        return jnp.concatenate([rows, jnp.zeros((LANES - rows.shape[0], LANES), jnp.float32)], axis=0)

    up_old_ref[...] = own_columns(up_rows_ref)
    dense_old_ref[...] = own_columns(qkv_rows_ref, out_rows_ref, moments_ref)
    around = down_rows_ref[:, pl.ds(pl.multiple_of(me // 2 * LANES, LANES), LANES)]
    both_halves = padded(around).T
    down_old_ref[...] = jnp.where(lax.rem(me, 2) == 0, both_halves[:own_down], both_halves[own_down:])
    dense_cols_ref[:, : qkv_cols_ref.shape[1]] = qkv_cols_ref[...]
    dense_cols_ref[:, qkv_cols_ref.shape[1] :] = out_cols_ref[...]

    def column_of(table_ref, lane, at):
        return jnp.sum(jnp.where(lane == at, table_ref[...], 0.0), axis=1, keepdims=True)

    up_lane = lax.broadcasted_iota(jnp.int32, (own_up, LANES), 1)
    down_lane = lax.broadcasted_iota(jnp.int32, (own_down, LANES), 1)
    up_new_ref[...] = jnp.zeros_like(up_new_ref)
    down_new_ref[...] = jnp.zeros_like(down_new_ref)

    def factored(grad, old):
        square = grad * grad
        new = decayed(old, jnp.mean(square + EPS_STAT, axis=1, keepdims=True))
        return (
            new,
            jnp.sum(square + EPS_STAT, axis=0, keepdims=True),
            jnp.sum(square * (1.0 / new), axis=0, keepdims=True),
        )

    def expert(values, at):
        for kind, (part, old_ref, new_ref, lane, rows) in enumerate(
            (
                (values[:own_up, :], up_old_ref, up_new_ref, up_lane, own_up),
                (values[own_up:, :], down_old_ref, down_new_ref, down_lane, own_down),
            )
        ):
            new, total, scaled = factored(part.astype(jnp.float32), column_of(old_ref, lane, at))
            new_ref[:rows, :] = jnp.where(lane == at, new, new_ref[:rows, :])
            for h in range(2):
                span = slice(h * wide, (h + 1) * wide)
                pay_s[at, 4 * kind + h : 4 * kind + h + 1, :] = total[:, span]
                pay_s[at, 4 * kind + 2 + h : 4 * kind + 3 + h, :] = scaled[:, span]

    own_at, got_at = pair_bit * half, (1 - pair_bit) * half

    def at_place(chosen, span):
        return tuple(chosen.get(bits - 1 - i, slice(None)) for i in range(bits)) + (
            chosen.get(bits, slice(None)),
            slice(None),
            span,
        )

    def got_place(step, span):
        return (slice(None),) * (steps - 1 - step) + (slice(None), span)

    loading.wait()
    chosen = [{} for _ in spans]
    for step in range(steps + 1):
        for part, span in enumerate(spans):
            flying[part].wait_recv()
            if step == 0:
                sum_ref[..., span] = plus(mine_ref[..., span], first_got[..., span])
            else:
                here = at_place(chosen[part], span)
                sum_ref[here] = plus(sum_ref[here], got[step - 1][got_place(step - 1, span)])
            if step < steps:
                link = orders[part][step]
                bit, peer = links[link]
                away = at_place({**chosen[part], link: 1 - bit}, span)
                flying[part] = push(sum_ref.at[away], got[step].at[got_place(step, span)], peer)
                chosen[part] = {**chosen[part], link: bit}
            else:
                dense_ref[core, chip, :, span] = sum_ref[at_place(chosen[part], span)]
                block = dense_ref.at[core, chip, :, span]
                flying[part] = push(block, block, chip_peer)
        if step == 0:
            expert(own_0, own_at)
            expert(got_0, got_at)
            expert(own_1, own_at + 1)
            expert(got_1, got_at + 1)
        elif step == 1:
            expert(ends_ref[0], own_at + 2)
        elif step == steps - 1:
            cross_2.wait_recv()
            expert(ends_ref[2], got_at + 2)
            far_exchange.wait_recv()
            go_s[1] = plus(far_stay_s[1 - pair_bit], far_got_s[1 - pair_bit])
            cross_3 = push(go_s.at[1], ends_ref.at[3], pair)
            ends_ref[1] = plus(far_stay_s[pair_bit], far_got_s[pair_bit])
            expert(ends_ref[1], own_at + 3)
    for part, span in enumerate(spans):
        flying[part].wait_recv()
        block = dense_ref.at[core, :, :, span]
        flying[part] = push(block, block, core_peer)
    cross_3.wait_recv()
    expert(ends_ref[3], got_at + 3)
    arriving = [push(pay_s.at[after[k]], got_s.at[k], {"dp": after[k]}) for k in range(1, count)]
    for copy in flying:
        copy.wait_recv()

    columns = dense_cols_ref.shape[1]
    piece = columns // count
    dense = dense_ref[...].reshape(own_up, dense_ref.shape[3])
    dense_lane = lax.broadcasted_iota(jnp.int32, dense_new_ref.shape, 1)
    old = dense_old_ref[...]
    qkv_columns = columns - width
    totals, scaleds, rows_new = [], [], []
    for at, span in enumerate((slice(0, qkv_columns), slice(qkv_columns, columns))):
        new, total, scaled = factored(
            dense[:, span].astype(jnp.float32), column_of(dense_old_ref, dense_lane, at)
        )
        rows_new.append(new)
        totals.append(total)
        scaleds.append(scaled)
    gain_lanes = (dense_lane == 2) | (dense_lane == 3)
    gains = pltpu.roll(dense[:, columns:].astype(jnp.float32), 2, 1)
    moments = jnp.where(gain_lanes, decayed(old, gains * gains + EPS_STAT), 1.0)
    gain_steps = jnp.where(gain_lanes, gains * lax.rsqrt(moments), 0.0)
    dense_new_ref[...] = jnp.where(
        dense_lane == 0,
        rows_new[0],
        jnp.where(dense_lane == 1, rows_new[1], jnp.where(gain_lanes, gain_steps, pltpu.roll(moments, 2, 1))),
    )
    gain_squares = jnp.sum(jnp.sum(gain_steps * gain_steps, axis=1, keepdims=True), axis=0, keepdims=True)
    total = jnp.concatenate(totals, axis=1)
    scaled = jnp.concatenate(scaleds, axis=1)
    for d in range(count):
        span = slice(d * piece, (d + 1) * piece)
        dense_pay_s[d] = jnp.concatenate(
            [total[:, span], scaled[:, span], jnp.broadcast_to(gain_squares, (1, piece)), jnp.zeros((5, piece), jnp.float32)],
            axis=0,
        )
    dense_arriving = [push(dense_pay_s.at[after[k]], dense_got_s.at[k], {"dp": after[k]}) for k in range(1, count)]

    tile = pay_s[me]
    for k in range(1, count):
        arriving[k - 1].wait_recv()
        tile = tile + got_s[k]
    made = []
    tops = []
    for kind, (rows_ref, cols_ref, rows) in enumerate(
        ((up_rows_ref, up_cols_ref, width), (down_rows_ref, down_cols_ref, ff))
    ):
        here = pl.ds(me, 1)
        square = jnp.concatenate([tile[4 * kind + h : 4 * kind + h + 1] for h in range(2)], axis=1)
        scaled = jnp.concatenate([tile[4 * kind + 2 + h : 4 * kind + 3 + h] for h in range(2)], axis=1)
        new_columns = decayed(cols_ref[here, :], square / rows)
        row_mean = decayed(
            jnp.mean(rows_ref[here, :], axis=1, keepdims=True),
            jnp.sum(square, axis=1, keepdims=True) / (rows * width),
        )
        squares = row_mean * jnp.sum(scaled / new_columns, axis=1, keepdims=True)
        made += [new_columns[:, :wide], new_columns[:, wide:]]
        tops += [jnp.broadcast_to(v, (1, wide)) for v in (row_mean, squares)]
    out_ref[me] = jnp.concatenate(made + tops, axis=0)
    arriving = [push(out_ref.at[me], out_ref.at[me], {"dp": after[k]}) for k in range(1, count)]

    tile = dense_pay_s[me]
    for k in range(1, count):
        dense_arriving[k - 1].wait_recv()
        tile = tile + dense_got_s[k]
    own_piece = pl.ds(pl.multiple_of(me * piece, LANES), piece)
    new_columns = decayed(dense_cols_ref[:, own_piece], tile[0:1] / width)
    is_qkv = lax.broadcasted_iota(jnp.int32, (1, piece), 1) + me * piece < qkv_columns
    ratio = tile[1:2] / new_columns
    sums = [
        jnp.sum(jnp.where(chosen_columns, row, 0.0), axis=1, keepdims=True)
        for row in (ratio, tile[0:1])
        for chosen_columns in (is_qkv, ~is_qkv)
    ]
    dense_out_ref[me] = jnp.concatenate(
        [new_columns]
        + [jnp.broadcast_to(v, (1, piece)) for v in sums]
        + [tile[2:3], jnp.zeros((2, piece), jnp.float32)],
        axis=0,
    )
    dense_arriving = [push(dense_out_ref.at[me], dense_out_ref.at[me], {"dp": after[k]}) for k in range(1, count)]

    for copy in arriving:
        copy.wait_recv()
    total = out_ref[0, :, :LANES]
    for a in range(1, count):
        total = total + out_ref[a, :, :LANES]
    spread_s[place] = total
    arriving = [push(spread_s.at[place], spread_s.at[place], {"expert": beside[k]}) for k in range(1, groups)]
    for copy in arriving + dense_arriving + [cross_mix]:
        copy.wait_recv()
    total = spread_s[0]
    for e in range(1, groups):
        total = total + spread_s[e]
    sums_ref[...] = total
    push.finish()


FAR = 4


def finish(dense, owns, gots, settling, mixes, statistics, label):
    count = lax.axis_size("dp")
    groups = lax.axis_size("expert")
    width, dense_width = dense.shape
    bits = count.bit_length() - 1
    quarter = width // count // 4
    parts = 6
    tiles = dense_width // LANES
    bounds = [LANES * (tiles * i // parts) for i in range(parts + 1)]
    spans = [slice(a, b) for a, b in zip(bounds[:-1], bounds[1:])]
    last = tuple(range(1, bits))
    orders = [((bits, 0) if part % 2 == 0 else (0, bits)) + last for part in range(parts)]
    half = (2,) * bits + (2, quarter, dense_width)
    rows = owns[0].shape[0]
    own_up, own_down = width // count, rows - width // count
    dense_columns = dense_width - LANES
    piece = dense_columns // count
    vmem = pl.BlockSpec(memory_space=pltpu.VMEM)
    stat_tiles = (count, 8, width // 2)
    dense_tiles = (count, 8, piece)
    copies = parts * (bits + 4) + 4 * (count - 1) + groups - 1 + 4
    shape = lambda *s: jax.ShapeDtypeStruct(s, jnp.float32)
    low = lambda *s: jax.ShapeDtypeStruct(s, jnp.bfloat16)
    held = lambda *s: pltpu.VMEM(s, jnp.bfloat16)
    outs = (
        low(2, 2, quarter, dense_width),
        low(4, rows, width),
        low(*mixes[0].shape[1:]),
        shape(*stat_tiles),
        shape(8, LANES),
        shape(LANES, LANES),
        shape(LANES, LANES),
        shape(*dense_tiles),
        shape(width // count, LANES),
    )
    args = (
        dense.reshape((2,) * bits + (2, 2, quarter, dense_width)),
        *owns, *gots, *settling, *mixes, *statistics,
    )
    own, *rest = pl.pallas_call(
        functools.partial(finish_kernel, count, groups, 4, orders, spans),
        out_shape=outs,
        in_specs=[pl.BlockSpec(memory_space=pl.ANY)] + [vmem] * (len(args) - 1),
        out_specs=[vmem] * len(outs),
        scratch_shapes=[held(*half), held(*half)]
        + [held(*((2,) * (bits - step)), quarter, dense_width) for step in range(bits + 1)]
        + [
            held(*half),
            pltpu.SemaphoreType.DMA,
            held(2, rows, width),
            held(2, rows, width),
            held(2, rows, width),
            held(2, rows, width),
            held(*mixes[0].shape[1:]),
            pltpu.VMEM(stat_tiles, jnp.float32),
            pltpu.VMEM(stat_tiles, jnp.float32),
            pltpu.VMEM(dense_tiles, jnp.float32),
            pltpu.VMEM(dense_tiles, jnp.float32),
            pltpu.VMEM((groups, 8, LANES), jnp.float32),
            pltpu.VMEM((own_up, LANES), jnp.float32),
            pltpu.VMEM((own_down, LANES), jnp.float32),
            pltpu.VMEM((own_up, LANES), jnp.float32),
            pltpu.VMEM((1, dense_columns), jnp.float32),
            pltpu.SemaphoreType.DMA((copies,)),
            pltpu.SemaphoreType.DMA((copies,)),
        ],
        compiler_params=pltpu.CompilerParams(
            collective_id=label, has_side_effects=True, vmem_limit_bytes=VM
        ),
        cost_estimate=lasts(75),
        name="finish",
    )(*args)
    return own.reshape(width // count, dense_width), *rest


def update_kernel(counts, half, early, s_ref, *refs):
    owns, gots = refs[:early], refs[early : 2 * early]
    (dense_ref, ends_ref, pair_mix_ref, tiles_ref, sums_ref, up_new_ref, down_new_ref, dense_tiles_ref, dense_new_ref,
     qkv_old_ref, out_old_ref, middle_ref, near_mix_ref, got_mix_ref, up_w_ref, down_w_ref, qkv_w_ref, out_w_ref,
     block_ref, up_out_ref, down_out_ref, up_rows_ref, down_rows_ref, up_cols_ref, down_cols_ref,
     qkv_out_ref, out_out_ref, qkv_cols_ref, out_cols_ref, qkv_rows_ref, out_rows_ref, gains_ref, moments_ref,
     rms_ref) = refs[2 * early :]
    block_ref[...] = middle_ref[...] + (
        near_mix_ref[0].astype(jnp.float32)
        + got_mix_ref[0].astype(jnp.float32)
        + pair_mix_ref[...].astype(jnp.float32)
    )
    late = half - early
    own_up = up_out_ref.shape[1]
    own_down = down_out_ref.shape[1]
    wide = tiles_ref.shape[2]
    pair_bit = s_ref[0]
    count = dense_tiles_ref.shape[0]
    dense_sums = dense_tiles_ref[0, :, 0:1]
    for a in range(1, count):
        dense_sums = dense_sums + dense_tiles_ref[a, :, 0:1]
    width = qkv_old_ref.shape[1]
    qkv_columns = qkv_out_ref.shape[1]
    row_means = []
    squares = [dense_tiles_ref[0, 5:6, 0:1]]
    for at, (old_ref, columns) in enumerate(((qkv_old_ref, qkv_columns), (out_old_ref, width))):
        row_means.append(
            decayed(
                jnp.mean(old_ref[...], axis=1, keepdims=True),
                dense_sums[3 + at : 4 + at] / (width * columns),
            )
        )
        squares.append(row_means[-1] * dense_sums[1 + at : 2 + at])
    squares += [sums_ref[5:6, 0:1], sums_ref[7:8, 0:1]]
    roots = [jnp.sqrt(square / number) for square, number in zip(squares, counts)]
    factors = [LEARN_RATE / jnp.maximum(1.0, root / CLIP_LEVEL) for root in roots]
    for i, root in enumerate(roots):
        rms_ref[i] = root[0, 0]

    up_table = up_new_ref[...]
    down_table = down_new_ref[...]
    lane = lax.broadcasted_iota(jnp.int32, up_table.shape, 1)

    def expert(ref, at):
        tile = tiles_ref[at]
        for kind, (table, weight_ref, out_ref, first, rows) in enumerate(
            (
                (up_table, up_w_ref, up_out_ref, 0, own_up),
                (down_table, down_w_ref, down_out_ref, own_up, own_down),
            )
        ):
            row_mean = tile[4 + 2 * kind : 5 + 2 * kind, 0:1]
            column = jnp.sum(jnp.where(lane == at, table, 0.0), axis=1, keepdims=True)[:rows]
            scale = factors[3 + kind] * lax.rsqrt(column / row_mean)
            for h in range(2):
                span = slice(h * wide, (h + 1) * wide)
                columns = lax.rsqrt(tile[2 * kind + h : 2 * kind + h + 1, :])
                out_ref[at, :, span] = (
                    weight_ref[at, :, span].astype(jnp.float32)
                    - ref[first : first + rows, span].astype(jnp.float32) * scale * columns
                )

    own_at, got_at = pair_bit * half, (1 - pair_bit) * half
    for j in range(early):
        expert(owns[j], own_at + j)
        expert(gots[j], got_at + j)
    for j in range(late):
        expert(ends_ref.at[j], own_at + early + j)
        expert(ends_ref.at[late + j], got_at + early + j)
    up_rows_ref[...] = up_table.T[: up_rows_ref.shape[0], :own_up]
    down_rows_ref[...] = down_table.T[: down_rows_ref.shape[0], :own_down]
    for a in range(up_cols_ref.shape[0]):
        for h in range(2):
            span = slice(h * wide, (h + 1) * wide)
            up_cols_ref[a : a + 1, span] = tiles_ref[a, h : h + 1, :]
            down_cols_ref[a : a + 1, span] = tiles_ref[a, 2 + h : 3 + h, :]

    table = dense_new_ref[...]
    scales = [
        factors[1 + at] * lax.rsqrt(table[:, at : at + 1] / row_means[at]) for at in range(2)
    ]
    piece = dense_tiles_ref.shape[2]
    for first in range(0, qkv_columns + width, LANES):
        at = 0 if first < qkv_columns else 1
        weight_ref, out_ref, cols_ref = (
            (qkv_w_ref, qkv_out_ref, qkv_cols_ref) if at == 0 else (out_w_ref, out_out_ref, out_cols_ref)
        )
        here = slice(first - at * qkv_columns, first - at * qkv_columns + LANES)
        within = first % piece
        columns = dense_tiles_ref[first // piece, 0:1, within : within + LANES]
        cols_ref[:, here] = columns
        out_ref[:, here] = weight_ref[:, here].astype(jnp.float32) - dense_ref[
            :, first : first + LANES
        ].astype(jnp.float32) * scales[at] * lax.rsqrt(columns)
    turned = table.T
    qkv_rows_ref[...] = turned[0:1]
    out_rows_ref[...] = turned[1:2]
    gains_ref[...] = -factors[0] * turned[2:4]
    moments_ref[...] = turned[4:6]


def update(owns, gots, finished, row_statistics, middle, mixes, up_w, down_w, qkv_w, out_w):
    count = lax.axis_size("dp")
    groups = lax.axis_size("expert")
    me = lax.axis_index("dp")
    experts, width, up_columns = up_w.shape
    ff = down_w.shape[1]
    qkv_columns = qkv_w.shape[1]
    own_up, own_down = width // count, ff // count
    counts = (
        float(2 * width),
        float(width * qkv_columns),
        float(width * width),
        float(groups * experts * width * up_columns),
        float(groups * experts * ff * width),
    )
    ends = finished[1]
    early = len(owns)
    whole = lambda *shape: pl.BlockSpec(shape, lambda g, s: (0,) * len(shape))
    shape = lambda *s: jax.ShapeDtypeStruct(s, jnp.float32)
    rows = own_up + own_down
    outs = [
        shape(*middle.shape),
        shape(experts, own_up, up_columns),
        shape(experts, own_down, width),
        shape(experts, own_up),
        shape(experts, own_down),
        shape(experts, up_columns),
        shape(experts, width),
        shape(own_up, qkv_columns),
        shape(own_up, width),
        shape(1, qkv_columns),
        shape(1, width),
        shape(1, own_up),
        shape(1, own_up),
        shape(2, own_up),
        shape(2, own_up),
        shape(len(counts)),
    ]
    return pl.pallas_call(
        functools.partial(update_kernel, counts, early + ends.shape[0] // 2, early),
        out_shape=outs,
        grid_spec=pltpu.PrefetchScalarGridSpec(
            num_scalar_prefetch=1,
            grid=(1,),
            in_specs=[whole(rows, width)] * (2 * early)
            + [whole(*a.shape) for a in (*finished, *row_statistics, middle, *mixes)]
            + [
                pl.BlockSpec((experts, own_up, up_columns), lambda g, s: (0, s[1], 0)),
                pl.BlockSpec((experts, own_down, width), lambda g, s: (0, s[1], 0)),
                pl.BlockSpec((own_up, qkv_columns), lambda g, s: (s[1], 0)),
                pl.BlockSpec((own_up, width), lambda g, s: (s[1], 0)),
            ],
            out_specs=[whole(*o.shape) for o in outs[:-1]] + [pl.BlockSpec(memory_space=pltpu.SMEM)],
        ),
        compiler_params=pltpu.CompilerParams(vmem_limit_bytes=VM),
        cost_estimate=lasts(6),
        name="update",
    )(
        jnp.stack([lax.rem(me // PAIR, 2), me]),
        *owns, *gots, *finished, *row_statistics, middle, *mixes, up_w, down_w, qkv_w, out_w,
    )


D = 1024
FF = 512
TOP = 8


def swap(values, axis, mask):
    count = lax.axis_size(axis)
    return lax.ppermute(values, axis, [(i, i ^ mask) for i in range(count)])


def swap_pair(values):
    return swap(values, "dp", PAIR)


def swap_chip(values):
    return swap(values, "expert", 2)


def swap_core(values):
    return swap(values, "expert", 1)


def plus(a, b):
    return (a.astype(jnp.float32) + b.astype(jnp.float32)).astype(jnp.bfloat16)


def halve(blocks, axis, mask):
    bit = lax.rem(lax.axis_index(axis) // mask, 2)
    keep = lax.dynamic_index_in_dim(blocks, bit, 1, keepdims=False)
    give = lax.dynamic_index_in_dim(blocks, 1 - bit, 1, keepdims=False)
    return keep, swap(give, axis, mask)


def reduce_dense_far(blocks):
    count = lax.axis_size("dp")
    width, columns = blocks.shape
    rows = width // count
    blocks = blocks.reshape(count, 2, 2, rows // 4, columns)
    keep, got = halve(jnp.moveaxis(blocks, 2, 1), "expert", 1)
    keep, got = halve(plus(keep, got), "expert", 2)
    blocks = plus(keep, got)
    low = 1
    while low < count:
        keep, got = halve(blocks.reshape((-1, 2, 1) + blocks.shape[1:]), "dp", low)
        blocks = plus(keep, got).reshape((-1,) + blocks.shape[1:])
        low *= 2
    mine = blocks[0]
    chip = lax.axis_index("expert") // 2
    core = lax.rem(lax.axis_index("expert"), 2)
    other = swap_chip(mine)
    both = jnp.where(chip == 0, jnp.stack([mine, other]), jnp.stack([other, mine]))
    across = swap_core(both)
    all_four = jnp.where(core == 0, jnp.stack([both, across], 1), jnp.stack([across, both], 1))
    return all_four.reshape(rows, columns)


def own_share(matrix, along):
    count = lax.axis_size("dp")
    width = matrix.shape[along] // count
    return lax.dynamic_slice_in_dim(matrix, lax.axis_index("dp") * width, width, along)


def factored(part, rows_old):
    square = part * part
    rows_new = decayed(rows_old, jnp.mean(square + EPS_STAT, axis=-1))
    return (
        rows_new,
        jnp.sum(square + EPS_STAT, axis=-2),
        jnp.sum(square / rows_new[..., None], axis=-2),
    )


def per_device(
    hidden_in,
    out_grad,
    segment_ids,
    parent_ids,
    positions,
    expert_ids,
    gate_weights,
    norm_gains,
    qkv_weight,
    out_weight,
    gate_up_weight,
    down_weight,
    gain_moment,
    qkv_rows,
    qkv_cols,
    out_rows,
    out_cols,
    gateup_rows,
    gateup_cols,
    down_rows,
    down_cols,
):
    rows_here = hidden_in.shape[0]
    dp_count = lax.axis_size("dp")
    groups = lax.axis_size("expert")
    experts_here = gate_up_weight.shape[0]
    total_experts = experts_here * groups
    capacity = 3 * rows_here * TOP // (2 * total_experts)
    half_experts = experts_here // 2
    dp_index = lax.axis_index("dp")
    pair_bit = lax.rem(dp_index // PAIR, 2)
    first_local = pair_bit * half_experts
    first_expert = lax.axis_index("expert") * experts_here + first_local

    weight_high = gate_weights.astype(jnp.bfloat16)
    weight_low = (gate_weights - weight_high.astype(jnp.float32)).astype(jnp.bfloat16)
    routing = jnp.concatenate([expert_ids.astype(jnp.bfloat16), weight_high, weight_low], axis=1).T
    routing = jnp.pad(routing, ((0, ROUTE_ROWS - routing.shape[0]), (0, D - rows_here)))
    grad_rows = jnp.concatenate([out_grad.astype(jnp.bfloat16), routing], axis=0)
    chip_grad_rows = swap_chip(grad_rows)
    pair_grad_rows = swap_pair(grad_rows)
    ids = jnp.stack([segment_ids, parent_ids, positions])
    normed, qkv, attended, lse, middle, normed_ffn = attend(
        hidden_in, ids, norm_gains, qkv_weight, out_weight
    )
    received, arrived, scale, code = gather_and_select(
        normed_ffn, grad_rows, chip_grad_rows, pair_grad_rows, capacity, experts_here, half_experts, TOP, 5
    )
    scalars = jnp.stack([first_local, lax.rem(dp_index, 2)])
    experts, chains = [], []

    def advance(j, after, come=None, passed=()):
        masks, stay, go = chains[j]
        come = swap(go, "dp", masks[0]) if come is None else come
        stay, go, *passed = settle(stay, come, masks[1], "%d_%d" % (j, masks[1]), after, passed)
        chains[j] = (masks[1:], stay, go)
        return (stay, *passed) if passed else stay

    masks = [1] + [1 << b for b in range(2, dp_count.bit_length() - 1)] + [PAIR]
    for j in range(half_experts):
        after = [experts[-1][2]] if experts else []
        if j == 3:
            after.append(advance(0, after))
        experts.append(
            run_expert(
                scalars, j, received, arrived, scale, gate_up_weight, down_weight, dp_count, after
            )
        )
        chains.append((masks, experts[j][0], experts[j][1]))
    mine, theirs = combine(code, [e[2] for e in experts], capacity, [])
    steps = [advance(1, [mine])]
    normed_f_grad, near_mix, far_mix, come = return_sums(
        code, mine, theirs, [e[3] for e in experts], capacity, chains[1][2], chains[1][0][0], 6, steps
    )
    steps = [normed_f_grad]
    steps.append(advance(0, steps))
    stay, far_mix = advance(2, steps[-1:], None, [far_mix])
    steps.append(stay)
    steps.append(advance(1, steps[-1:], come))
    input_grad, dense = attend_back(
        hidden_in, out_grad, middle, normed_f_grad, normed, qkv, attended, lse, ids, norm_gains, qkv_weight,
        out_weight, steps
    )
    got_mix = swap_chip(far_mix)
    qkv_columns = qkv_weight.shape[1]
    fast_tail = dp_count == experts_here and D // dp_count % 64 == 0
    if fast_tail:
        owns = [chains[j][1][0] for j in (0, 1)]
        gots = [swap_pair(chains[j][2][0]) for j in (0, 1)]
        settling = []
        for j in (2, 3):
            masks, stay, go = chains[j]
            settling += [stay, swap(go, "dp", masks[0])]
        settling[2:] = [x.reshape((2, 2) + x.shape[1:]) for x in settling[2:]]
        finished = finish(
            dense,
            owns,
            gots,
            settling,
            (near_mix, got_mix),
            (
                gateup_rows,
                down_rows,
                gateup_cols,
                down_cols,
                qkv_rows[None],
                out_rows[None],
                gain_moment,
                qkv_cols[None],
                out_cols[None],
            ),
            1,
        )
        (
            block_out,
            gate_up_new,
            down_new,
            gateup_rows_new,
            down_rows_new,
            gateup_cols_new,
            down_cols_new,
            qkv_new,
            out_new,
            qkv_cols_new,
            out_cols_new,
            qkv_rows_new,
            out_rows_new,
            gains_update,
            gain_moment_new,
            update_rms,
        ) = update(
            owns,
            gots,
            finished,
            (qkv_rows[None], out_rows[None]),
            middle,
            (near_mix, got_mix),
            gate_up_weight,
            down_weight,
            qkv_weight,
            out_weight,
        )
        qkv_cols_new, out_cols_new = qkv_cols_new[0], out_cols_new[0]
        qkv_rows_new, out_rows_new = qkv_rows_new[0], out_rows_new[0]
    else:
        for_pair = settle_mix(near_mix, got_mix, [input_grad])
        mix_parts = (near_mix[0], got_mix[0], swap_pair(for_pair))
        block_out = middle + sum(part.astype(jnp.float32) for part in mix_parts)
        dense_own = reduce_dense_far(dense)
        for j in range(half_experts):
            while len(chains[j][0]) > 1:
                advance(j, [dense_own])
        own_parts = [c[1][0] for c in chains]
        other_parts = [swap_pair(c[2][0]) for c in chains]
        own = jnp.stack(own_parts).astype(jnp.float32)
        other = jnp.stack(other_parts).astype(jnp.float32)
        parts = jnp.where(pair_bit == 0, jnp.concatenate([own, other]), jnp.concatenate([other, own]))
        gateup_part = parts[:, : D // dp_count]
        down_part = parts[:, D // dp_count :]
        gateup_rows_new, gateup_square, gateup_scaled = factored(gateup_part, own_share(gateup_rows, 1))
        down_rows_new, down_square, down_scaled = factored(down_part, own_share(down_rows, 1))
        sizes = [gateup_square.size, gateup_scaled.size, down_square.size, down_scaled.size]
        summed = total_over(
            jnp.concatenate(
                [
                    gateup_square.reshape(-1),
                    gateup_scaled.reshape(-1),
                    down_square.reshape(-1),
                    down_scaled.reshape(-1),
                    jnp.sum(gateup_rows_new, axis=1),
                    jnp.sum(down_rows_new, axis=1),
                ]
            ),
            "dp",
            1,
        )
        pieces = jnp.split(summed, [sum(sizes[: i + 1]) for i in range(4)])
        gateup_square, gateup_scaled, down_square, down_scaled = [
            p.reshape(experts_here, D) for p in pieces[:4]
        ]
        gateup_row_mean = pieces[4][:experts_here] / D
        down_row_mean = pieces[4][experts_here:] / FF
        gateup_cols_new = decayed(gateup_cols, gateup_square / D)
        down_cols_new = decayed(down_cols, down_square / FF)
        expert_squares = jnp.stack(
            [
                jnp.sum(gateup_row_mean * jnp.sum(gateup_scaled / gateup_cols_new, axis=1)),
                jnp.sum(down_row_mean * jnp.sum(down_scaled / down_cols_new, axis=1)),
            ]
        )
        spread_squares = collect(
            jnp.zeros((8, 128), jnp.float32).at[0, :2].set(expert_squares), "expert", 2
        )
        expert_squares = jnp.sum(spread_squares[:, 0, :2], axis=0)
        dense_own = dense_own.astype(jnp.float32)
        qkv_own = dense_own[:, :qkv_columns]
        out_own = dense_own[:, qkv_columns : qkv_columns + D]
        gains_own = dense_own[:, qkv_columns + D : qkv_columns + D + 2].T
        gain_moment_new = decayed(own_share(gain_moment, 1), gains_own * gains_own + EPS_STAT)
        gains_step = gains_own * lax.rsqrt(gain_moment_new)
        qkv_rows_new, qkv_square, qkv_scaled = factored(qkv_own, own_share(qkv_rows, 0))
        out_rows_new, out_square, out_scaled = factored(out_own, own_share(out_rows, 0))
        dense_sums = total_over(
            jnp.concatenate(
                [
                    qkv_square,
                    qkv_scaled,
                    out_square,
                    out_scaled,
                    jnp.stack(
                        [jnp.sum(qkv_rows_new), jnp.sum(out_rows_new), jnp.sum(gains_step * gains_step)]
                    ),
                ]
            ),
            "dp",
            4,
        )
        qkv_square, qkv_scaled, out_square, out_scaled, rest = jnp.split(
            dense_sums, [qkv_columns, 2 * qkv_columns, 2 * qkv_columns + D, 2 * qkv_columns + 2 * D]
        )
        qkv_row_mean = rest[0] / D
        out_row_mean = rest[1] / D
        qkv_cols_new = decayed(qkv_cols, qkv_square / D)
        out_cols_new = decayed(out_cols, out_square / D)
        squares = jnp.concatenate(
            [
                jnp.stack(
                    [
                        rest[2],
                        qkv_row_mean * jnp.sum(qkv_scaled / qkv_cols_new),
                        out_row_mean * jnp.sum(out_scaled / out_cols_new),
                    ]
                ),
                expert_squares,
            ]
        )
        element_counts = jnp.array(
            [2 * D, D * qkv_columns, D * D, total_experts * D * 2 * FF, total_experts * FF * D], jnp.float32
        )
        update_rms = jnp.sqrt(squares / element_counts)
        factors = LEARN_RATE / jnp.maximum(1.0, update_rms / CLIP_LEVEL)

        def stepped(weight, part, rows_new, row_mean, cols_new, factor):
            return weight.astype(jnp.float32) - part * (
                factor * lax.rsqrt(rows_new / row_mean[..., None])
            )[..., :, None] * lax.rsqrt(cols_new)[..., None, :]

        gains_update = -factors[0] * gains_step
        qkv_new = stepped(own_share(qkv_weight, 0), qkv_own, qkv_rows_new, qkv_row_mean, qkv_cols_new, factors[1])
        out_new = stepped(own_share(out_weight, 0), out_own, out_rows_new, out_row_mean, out_cols_new, factors[2])
        gate_up_new = stepped(
            own_share(gate_up_weight, 1), gateup_part, gateup_rows_new, gateup_row_mean, gateup_cols_new, factors[3]
        )
        down_new = stepped(
            own_share(down_weight, 1), down_part, down_rows_new, down_row_mean, down_cols_new, factors[4]
        )
    return (
        block_out,
        input_grad,
        update_rms,
        gains_update,
        gain_moment_new,
        qkv_new,
        qkv_rows_new,
        qkv_cols_new,
        out_new,
        out_rows_new,
        out_cols_new,
        gate_up_new,
        gateup_rows_new,
        gateup_cols_new,
        down_new,
        down_rows_new,
        down_cols_new,
    )


def solution(mesh):
    placed = (
        P(("dp", "expert"), None),
        P(("dp", "expert"), None),
        P(("dp", "expert")),
        P(("dp", "expert")),
        P(("dp", "expert")),
        P(("dp", "expert"), None),
        P(("dp", "expert"), None),
        P(),
        P(),
        P(),
        P("expert", None, None),
        P("expert", None, None),
        P(),
        P(),
        P(),
        P(),
        P(),
        P("expert", None),
        P("expert", None),
        P("expert", None),
        P("expert", None),
    )
    return jax.shard_map(
        per_device,
        mesh=mesh,
        in_specs=placed,
        out_specs=(
            P(("dp", "expert"), None),
            P(("dp", "expert"), None),
            P(),
            P(None, "dp"),
            P(None, "dp"),
            P("dp", None),
            P("dp"),
            P(),
            P("dp", None),
            P("dp"),
            P(),
            P("expert", "dp", None),
            P("expert", "dp"),
            P("expert", None),
            P("expert", "dp", None),
            P("expert", "dp"),
            P("expert", None),
        ),
        check_vma=False,
    )
```

profile of v0, /device:TPU:0, one launch (start us, length us, event | category | flops | bytes accessed | tf_op | source)
XLA Modules:
  0.0 372.8 jit_solution(5606207168160311981)
XLA Ops:
  2.2 1.5 convert_element_type.17
  3.8 3.1 collective-permute-start.1
  9.1 17.8 %attend.1 = (bf16[384,1024]{1,0:T(8,128)(2,1)}, bf16[384,2048]{1,0:T(8,128)(2,1)}, bf16[384,1024]{1,0:T(8,128)(2,1)}, f32[384,128]{1,0:T(8,128)}, f32[384,1024]{1,0:T(8,128)}, /*index=5*/bf16[384,1024]{1,0:T(8,128)(2,1)}) custom-call(f32[384,1024]{1,0:T(8,128)} %hidden_hbm.1, s32[3,384]{1,0:T(4,128)} %pad_add_fusion.ids_ref, bf16[2,1024]{1,0:T(2,128)(2,1)} %gains_ref.3, ...), custom_call_target="tpu_custom_call" | custom-call | flops 18000000 | bytes 1024 | tf_op jit(solution)/shard_map/attend/pallas_call | solution.py:285
  28.6 44.6 %gather_and_select.1 = (bf16[4,8,144,1024]{3,2,1,0:T(8,128)(2,1)}, bf16[4,8,144,1024]{3,2,1,0:T(8,128)(2,1)}, f32[4,8,144,1]{3,2,1,0:T(8,128)}, f32[8,4,384]{2,1,0:T(4,128)}) custom-call(bf16[384,1024]{1,0:T(8,128)(2,1)} %get-tuple-element.87.token_ref, bf16[416,1024]{1,0:T(8,128)(2,1)} %copy-done.1, bf16[416,1024]{1,0:T(8,128)(2,1)} %copy-done.8, ...), custom_call_target="tpu_custom_call" | custom-call | flops 44000000 | bytes 1024 | tf_op jit(solution)/shard_map/gather_and_select/pallas_call | solution.py:730
  73.2 18.8 %expert_0.1 = (bf16[4,192,1024]{2,1,0:T(8,128)(2,1)}, bf16[4,192,1024]{2,1,0:T(8,128)(2,1)}, bf16[1152,1024]{1,0:T(8,128)(2,1)}, bf16[1152,1024]{1,0:T(8,128)(2,1)}) custom-call(s32[2]{0:T(128)} %pad_add_fusion.2.s_ref, bf16[4,8,144,1024]{3,2,1,0:T(8,128)(2,1)} %get-tuple-element.88.rec_hbm, bf16[4,8,144,1024]{3,2,1,0:T(8,128)(2,1)} %get-tuple-element.89.arr_hbm, ...), custom_call_target="tpu_custom_call" | custom-call | flops 18000000 | bytes 1024 | tf_op jit(solution)/shard_map/expert_0/pallas_call | solution.py:121
  92.1 1.6 collective-permute-start.2
  93.6 18.5 %expert_1.1 = (bf16[4,192,1024]{2,1,0:T(8,128)(2,1)}, bf16[4,192,1024]{2,1,0:T(8,128)(2,1)}, bf16[1152,1024]{1,0:T(8,128)(2,1)}, bf16[1152,1024]{1,0:T(8,128)(2,1)}) custom-call(s32[2]{0:T(128)} %pad_add_fusion.2.s_ref, bf16[4,8,144,1024]{3,2,1,0:T(8,128)(2,1)} %get-tuple-element.88.rec_hbm, bf16[4,8,144,1024]{3,2,1,0:T(8,128)(2,1)} %get-tuple-element.89.arr_hbm, ...), custom_call_target="tpu_custom_call" | custom-call | flops 18000000 | bytes 1024 | tf_op jit(solution)/shard_map/expert_1/pallas_call | solution.py:121
  112.8 18.9 %expert_2.1 = (bf16[4,192,1024]{2,1,0:T(8,128)(2,1)}, bf16[4,192,1024]{2,1,0:T(8,128)(2,1)}, bf16[1152,1024]{1,0:T(8,128)(2,1)}, bf16[1152,1024]{1,0:T(8,128)(2,1)}) custom-call(s32[2]{0:T(128)} %pad_add_fusion.2.s_ref, bf16[4,8,144,1024]{3,2,1,0:T(8,128)(2,1)} %get-tuple-element.88.rec_hbm, bf16[4,8,144,1024]{3,2,1,0:T(8,128)(2,1)} %get-tuple-element.89.arr_hbm, ...), custom_call_target="tpu_custom_call" | custom-call | flops 18000000 | bytes 1024 | tf_op jit(solution)/shard_map/expert_2/pallas_call | solution.py:121
  131.7 1.6 collective-permute-start.5
  134.4 3.3 settle_0_4.1
  137.7 2.6 collective-permute-start.3
  140.4 18.4 %expert_3.1 = (bf16[4,192,1024]{2,1,0:T(8,128)(2,1)}, bf16[4,192,1024]{2,1,0:T(8,128)(2,1)}, bf16[1152,1024]{1,0:T(8,128)(2,1)}, bf16[1152,1024]{1,0:T(8,128)(2,1)}) custom-call(s32[2]{0:T(128)} %pad_add_fusion.2.s_ref, bf16[4,8,144,1024]{3,2,1,0:T(8,128)(2,1)} %get-tuple-element.88.rec_hbm, bf16[4,8,144,1024]{3,2,1,0:T(8,128)(2,1)} %get-tuple-element.89.arr_hbm, ...), custom_call_target="tpu_custom_call" | custom-call | flops 18000000 | bytes 1024 | tf_op jit(solution)/shard_map/expert_3/pallas_call | solution.py:121
  159.5 10.6 %combine.1 = (bf16[4,384,1024]{2,1,0:T(8,128)(2,1)}, bf16[4,384,1024]{2,1,0:T(8,128)(2,1)}) custom-call(f32[8,4,384]{2,1,0:T(4,128)} %get-tuple-element.98.code_ref, bf16[1152,1024]{1,0:T(8,128)(2,1)} %get-tuple-element.93.refs_0_, bf16[1152,1024]{1,0:T(8,128)(2,1)} %get-tuple-element.94.refs_0_.refs_1_, ...), custom_call_target="tpu_custom_call" | custom-call | flops 12000000 | bytes 1024 | tf_op jit(solution)/shard_map/combine/pallas_call | solution.py:808
  170.1 3.3 settle_1_4.1
  173.4 52.2 %return_sums.1 = (f32[384,1024]{1,0:T(8,128)}, bf16[2,384,1024]{2,1,0:T(8,128)(2,1)}, bf16[2,384,1024]{2,1,0:T(8,128)(2,1)}, bf16[2,192,1024]{2,1,0:T(8,128)(2,1)}) custom-call(f32[8,4,384]{2,1,0:T(4,128)} %get-tuple-element.98.code_ref, bf16[4,384,1024]{2,1,0:T(8,128)(2,1)} %get-tuple-element.100.refs_0_.mine_ref, ...), custom_call_target="tpu_custom_call" | custom-call | flops 37000000 | bytes 1024 | tf_op jit(solution)/shard_map/return_sums/pallas_call | solution.py:888
  225.6 2.4 settle_0_2.1
  229.1 3.3 settle_2_4.1
  232.5 1.8 collective-permute-start.10
  234.5 2.7 collective-permute-start.6
  237.2 2.4 settle_1_2.1
  240.2 22.9 %attend_back.1 = (f32[384,1024]{1,0:T(8,128)}, bf16[1024,3200]{1,0:T(8,128)(2,1)}) custom-call(f32[384,1024]{1,0:T(8,128)} %grad_ref.1, f32[384,1024]{1,0:T(8,128)} %get-tuple-element.120.middle_ref.refs_15_, f32[384,1024]{1,0:T(8,128)} %get-tuple-element.110.refs_0_.normed_grad_ref, f32[384,128]{1,0:T(8,128)} %get-tuple-element.121.lse_ref, ...), custom_call_target="tpu_custom_call" | custom-call | flops 26000000 | bytes 1024 | tf_op jit(solution)/shard_map/attend_back/pallas_call | solution.py:434
  263.1 8.5 %collective-permute-done.7.refs_4_.refs_3_ = bf16[192,1024]{1,0:T(8,128)(2,1)S(1)} collective-permute-done((bf16[192,1024]{1,0:T(8,128)(2,1)}, bf16[192,1024]{1,0:T(8,128)(2,1)S(1)}, u32[]{:S(2)}, u32[]{:S(2)}) %collective-permute-start.7) | collective-permute-done | bytes 393248 | tf_op jit(solution)/shard_map/ppermute | solution.py:1484
  273.4 88.1 %finish.1 = (bf16[2,2,32,3200]{3,2,1,0:T(8,128)(2,1)}, bf16[4,192,1024]{2,1,0:T(8,128)(2,1)}, bf16[384,1024]{1,0:T(8,128)(2,1)}, f32[8,8,512]{2,1,0:T(8,128)}, f...) custom-call(bf16[2,2,2,2,2,32,3200]{6,5,4,3,2,1,0:T(8,128)(2,1)} %bi, ...), custom_call_target="tpu_custom_call" | custom-call | flops 75000000 | bytes 1024 | tf_op jit(solution)/shard_map/finish/pallas_call | solution.py:1277
  361.4 11.0 %update.1 = (f32[384,1024]{1,0:T(8,128)}, f32[8,128,1024]{2,1,0:T(8,128)}, f32[8,64,1024]{2,1,0:T(8,128)}, f32[8,128]{1,0:T(8,128)}, f32[8,64]{1,0:T(8,128)}, /*...) custom-call(s32[2]{0:T(128)} %pad_add_fusion.1.s_ref, ...), custom_call_target="tpu_custom_call" | custom-call | flops 6000000 | bytes 1024 | tf_op jit(solution)/shard_map/update/pallas_call | solution.py:1452
  (49 shorter events, 11.7 us)
Async XLA Ops:
  2.2 6.3 %copy-start.9 = (s32[384]{0:T(512)S(1)}, s32[384]{0:T(512)}, u32[]{:S(2)}) copy-start(s32[384]{0:T(512)} %param.23) | copy-start | bytes 4612
  2.2 6.3 %copy-start.10 = (s32[384]{0:T(512)S(1)}, s32[384]{0:T(512)}, u32[]{:S(2)}) copy-start(s32[384]{0:T(512)} %param.24) | copy-start | bytes 4612
  2.2 6.3 %copy-start.11 = (s32[384]{0:T(512)S(1)}, s32[384]{0:T(512)}, u32[]{:S(2)}) copy-start(s32[384]{0:T(512)} %param.25) | copy-start | bytes 4612
  3.8 23.1 %copy-start.1 = (bf16[416,1024]{1,0:T(8,128)(2,1)}, bf16[416,1024]{1,0:T(8,128)(2,1)S(1)}, u32[]{:S(2)}) copy-start(bf16[416,1024]{1,0:T(8,128)(2,1)S(1)} %fusion.1.grad_ref) | copy-start | bytes 2555908
  3.8 23.6 %collective-permute-start.1 = (bf16[416,1024]{1,0:T(8,128)(2,1)S(1)}, bf16[416,1024]{1,0:T(8,128)(2,1)S(1)}, u32[]{:S(2)}, u32[]{:S(2)}) collective-permute-start(bf16[416,1024]{1,0:T(8,128)(2,1)S(1)} %fusion.1.grad_ref), channel_id=1, source_target_pairs={{0,8},{4,12},{8,0},{12,4},{16,24},{20,28},{24,16},{28,20},{1,9},{5... | collective-permute-start | bytes 2555912 | tf_op jit(solution)/shard_map/ppermute | solution.py:1484
  6.9 20.6 %collective-permute-start = (bf16[416,1024]{1,0:T(8,128)(2,1)S(1)}, bf16[416,1024]{1,0:T(8,128)(2,1)S(1)}, u32[]{:S(2)}, u32[]{:S(2)}) collective-permute-start(bf16[416,1024]{1,0:T(8,128)(2,1)S(1)} %fusion.1.grad_ref), channel_id=1, source_target_pairs={{0,2},{1,3},{2,0},{3,1},{4,6},{5,7},{6,4},{7,5},{8,10},{9,11},{10,... | collective-permute-start | bytes 2555912 | tf_op jit(solution)/shard_map/ppermute | solution.py:1484
  27.5 0.9 copy-start.7
  27.5 1.2 copy-start.8
  92.1 41.2 %collective-permute-start.2 = (bf16[4,192,1024]{2,1,0:T(8,128)(2,1)}, bf16[4,192,1024]{2,1,0:T(8,128)(2,1)S(1)}, u32[]{:S(2)}, u32[]{:S(2)}) collective-permute-start(bf16[4,192,1024]{2,1,0:T(8,128)(2,1)} %get-tuple-element.92), channel_id=1, source_target_pairs={{0,4},{4,0},{8,12},{12,8},{16,20},{20,16},{24,28},{28,24},{1,5},{5... | collective-permute-start | bytes 4718600 | tf_op jit(solution)/shard_map/ppermute | solution.py:1484
  112.2 57.9 %collective-permute-start.4 = (bf16[4,192,1024]{2,1,0:T(8,128)(2,1)}, bf16[4,192,1024]{2,1,0:T(8,128)(2,1)}, u32[]{:S(2)}, u32[]{:S(2)}) collective-permute-start(bf16[4,192,1024]{2,1,0:T(8,128)(2,1)} %get-tuple-element.103), channel_id=1, source_target_pairs={{0,4},{4,0},{8,12},{12,8},{16,20},{20,16},{24,28},{28,24},{1,5},{5... | collective-permute-start | bytes 4718600 | tf_op jit(solution)/shard_map/ppermute | solution.py:1484
  131.7 96.3 %collective-permute-start.5 = (bf16[4,192,1024]{2,1,0:T(8,128)(2,1)}, bf16[4,192,1024]{2,1,0:T(8,128)(2,1)S(1)}, u32[]{:S(2)}, u32[]{:S(2)}) collective-permute-start(bf16[4,192,1024]{2,1,0:T(8,128)(2,1)} %get-tuple-element.114), channel_id=1, source_target_pairs={{0,4},{4,0},{8,12},{12,8},{16,20},{20,16},{24,28},{28,24},{1,5},{5... | collective-permute-start | bytes 4718600 | tf_op jit(solution)/shard_map/ppermute | solution.py:1484
  133.2 1.1 copy-start.6
  137.7 87.9 %collective-permute-start.3 = (bf16[2,192,1024]{2,1,0:T(8,128)(2,1)}, bf16[2,192,1024]{2,1,0:T(8,128)(2,1)}, u32[]{:S(2)}, u32[]{:S(2)}) collective-permute-start(bf16[2,192,1024]{2,1,0:T(8,128)(2,1)} %bitcast.72), channel_id=1, source_target_pairs={{0,16},{4,20},{8,24},{12,28},{16,0},{20,4},{24,8},{28,12},{1,17},{... | collective-permute-start | bytes 2359304 | tf_op jit(solution)/shard_map/ppermute | solution.py:1484
  158.7 112.9 %collective-permute-start.9 = (bf16[4,192,1024]{2,1,0:T(8,128)(2,1)}, bf16[4,192,1024]{2,1,0:T(8,128)(2,1)S(1)}, u32[]{:S(2)}, u32[]{:S(2)}) collective-permute-start(bf16[4,192,1024]{2,1,0:T(8,128)(2,1)} %get-tuple-element.128), channel_id=1, source_target_pairs={{0,4},{4,0},{8,12},{12,8},{16,20},{20,16},{24,28},{28,24},{1,5},{5... | collective-permute-start | bytes 4718600 | tf_op jit(solution)/shard_map/ppermute | solution.py:1484
  228.0 1.1 copy-start.5
  232.5 39.1 %collective-permute-start.10 = (bf16[2,384,1024]{2,1,0:T(8,128)(2,1)}, bf16[2,384,1024]{2,1,0:T(8,128)(2,1)S(1)}, u32[]{:S(2)}, u32[]{:S(2)}) collective-permute-start(bf16[2,384,1024]{2,1,0:T(8,128)(2,1)} %get-tuple-element.130), channel_id=1, source_target_pairs={{0,2},{1,3},{2,0},{3,1},{4,6},{5,7},{6,4},{7,5},{8,10},{9,11},{10,... | collective-permute-start | bytes 4718600 | tf_op jit(solution)/shard_map/ppermute | solution.py:1484
  234.3 37.3 %collective-permute-start.8 = (bf16[2,192,1024]{2,1,0:T(8,128)(2,1)}, bf16[2,192,1024]{2,1,0:T(8,128)(2,1)}, u32[]{:S(2)}, u32[]{:S(2)}) collective-permute-start(bf16[2,192,1024]{2,1,0:T(8,128)(2,1)} %bitcast.73), channel_id=1, source_target_pairs={{0,16},{4,20},{8,24},{12,28},{16,0},{20,4},{24,8},{28,12},{1,17},{... | collective-permute-start | bytes 2359304 | tf_op jit(solution)/shard_map/ppermute | solution.py:1484
  234.5 28.7 %collective-permute-start.6 = (bf16[192,1024]{1,0:T(8,128)(2,1)}, bf16[192,1024]{1,0:T(8,128)(2,1)S(1)}, u32[]{:S(2)}, u32[]{:S(2)}) collective-permute-start(bf16[192,1024]{1,0:T(8,128)(2,1)} %bitcast.74), channel_id=1, source_target_pairs={{0,8},{4,12},{8,0},{12,4},{16,24},{20,28},{24,16},{28,20},{1,9},{5... | collective-permute-start | bytes 1179656 | tf_op jit(solution)/shard_map/ppermute | solution.py:1484
  239.5 32.0 %collective-permute-start.7 = (bf16[192,1024]{1,0:T(8,128)(2,1)}, bf16[192,1024]{1,0:T(8,128)(2,1)S(1)}, u32[]{:S(2)}, u32[]{:S(2)}) collective-permute-start(bf16[192,1024]{1,0:T(8,128)(2,1)} %bitcast.75), channel_id=1, source_target_pairs={{0,8},{4,12},{8,0},{12,4},{16,24},{20,28},{24,16},{28,20},{1,9},{5... | collective-permute-start | bytes 1179656 | tf_op jit(solution)/shard_map/ppermute | solution.py:1484
  263.1 8.5 %copy-start.2 = (bf16[192,1024]{1,0:T(8,128)(2,1)}, bf16[192,1024]{1,0:T(8,128)(2,1)S(1)}, u32[]{:S(2)}) copy-start(bf16[192,1024]{1,0:T(8,128)(2,1)S(1)} %collective-permute-done.6.refs_3_.refs_2_) | copy-start | bytes 1179652
  271.6 0.8 copy-start.3
  271.6 1.3 copy-start.4
  271.6 1.8 copy-start
where the time goes:
time: 377 us; the launch traced here: 373 us
  Pallas kernels  336 us (89%)
  starting transfers between devices  16.5 us (4%)
  waiting for transfers between devices  8.48 us (2%)
  local copies, waits for them, and re-layouts  5.23 us (1%)
  other arithmetic  4.9 us (1%)
    pallas_call x1, Pallas kernels, finish(): pl.pallas_call(functools.partial(finish_kernel, count, groups, 4, orders,...  88.1 us
    pallas_call x4, Pallas kernels, run_expert(): pl.pallas_call(functools.partial(expert_kernel, j, owners, tiles, len(aft...  74.6 us
    pallas_call x1, Pallas kernels, return_sums(): pl.pallas_call(functools.partial(return_kernel, capacity, count, far_mask...  52.2 us
    pallas_call x1, Pallas kernels, gather_and_select(): pl.pallas_call(functools.partial(gather_kernel, capacity, experts_here, h...  44.6 us
    pallas_call x1, Pallas kernels, attend_back(): pl.pallas_call(functools.partial(attend_back_kernel, len(after)), out_sha...  22.9 us
    pallas_call x1, Pallas kernels, attend(): pl.pallas_call(attend_kernel, out_shape=(shape((rows, width), jnp.bfloat1...  17.8 us
    ppermute x11, starting transfers between devices, swap(): return lax.ppermute(values, axis, [(i, i ^ mask) for i in range(count)])  16.5 us
    pallas_call x5, Pallas kernels, settle(): pl.pallas_call(functools.partial(settle_kernel, len(after) + len(passed))...  14.7 us
  transfers between devices with their start and end apart: 11, of which 1 were waited for; matrix products, arithmetic and copies ran while one was open for 0% of the time, Pallas kernels for 47%

commit v1 on v0

--- a/solution.py
+++ b/solution.py
@@ -911,51 +911,52 @@
     )(code, mine, theirs, go, *mixes, *after)
 
 
-def settle_kernel(waits, bit_ref, keep_hbm, got_hbm, *refs):
-    stay_ref, go_ref = refs[waits : waits + 2]
-    keep_ref, got_ref, sem = refs[-3:]
-    arriving = [
-        pltpu.make_async_copy(src, dst, sem.at[i])
-        for i, (src, dst) in enumerate(((keep_hbm, keep_ref), (got_hbm, got_ref)))
-    ]
+def settle_kernel(groups, waits, bits_ref, *refs):
+    ins, outs = refs[: 2 * groups], refs[2 * groups + waits : 4 * groups + waits]
+    held, sem = refs[-2 * groups - 1 : -1], refs[-1]
+    arriving = [pltpu.make_async_copy(ins[i], held[i], sem.at[i]) for i in range(2 * groups)]
     for copy in arriving:
         copy.start()
-    for copy in arriving:
-        copy.wait()
-    bit = bit_ref[0]
-    for high in range(keep_ref.shape[0]):
-        for low in range(keep_ref.shape[2]):
-            for ref, side in ((stay_ref, bit), (go_ref, 1 - bit)):
-                total = keep_ref[high, side, low].astype(jnp.float32) + got_ref[
-                    high, side, low
-                ].astype(jnp.float32)
-                ref[high, low] = total.astype(jnp.bfloat16)
-
-
-def settle(keep, got, mask, label, after, passed=()):
-    count, rows, columns = keep.shape
-    low = 1 if mask == PAIR else 2
-    shape = (count // 2 // low, 2, low, rows, columns)
-    half = jax.ShapeDtypeStruct((count // 2 // low, low, rows, columns), jnp.bfloat16)
-    bit = lax.rem(lax.axis_index("dp") // mask, 2)
+    for g in range(groups):
+        arriving[2 * g].wait()
+        arriving[2 * g + 1].wait()
+        keep_ref, got_ref, stay_ref, go_ref = held[2 * g], held[2 * g + 1], outs[2 * g], outs[2 * g + 1]
+        bit = bits_ref[g]
+        for high in range(keep_ref.shape[0]):
+            for low in range(keep_ref.shape[2]):
+                for ref, side in ((stay_ref, bit), (go_ref, 1 - bit)):
+                    total = keep_ref[high, side, low].astype(jnp.float32) + got_ref[
+                        high, side, low
+                    ].astype(jnp.float32)
+                    ref[high, low] = total.astype(jnp.bfloat16)
+
+
+def settle(groups, label, after, passed=()):
+    ins, shapes, outs, bits = [], [], [], []
+    for keep, got, mask in groups:
+        count, rows, columns = keep.shape
+        low = 1 if mask == PAIR else 2
+        shapes += [(count // 2 // low, 2, low, rows, columns)] * 2
+        ins += [keep.reshape(shapes[-1]), got.reshape(shapes[-1])]
+        outs += [jax.ShapeDtypeStruct((count // 2 // low, low, rows, columns), jnp.bfloat16)] * 2
+        bits.append(lax.rem(lax.axis_index("dp") // mask, 2))
+    waits = len(after) + len(passed)
     vmem = pl.BlockSpec(memory_space=pltpu.VMEM)
     anywhere = pl.BlockSpec(memory_space=pl.ANY)
-    stay, go, *passed = pl.pallas_call(
-        functools.partial(settle_kernel, len(after) + len(passed)),
-        out_shape=[half, half] + [jax.ShapeDtypeStruct(p.shape, p.dtype) for p in passed],
-        in_specs=[pl.BlockSpec(memory_space=pltpu.SMEM)] + [anywhere] * (2 + len(after) + len(passed)),
-        scratch_shapes=[
-            pltpu.VMEM(shape, jnp.bfloat16),
-            pltpu.VMEM(shape, jnp.bfloat16),
-            pltpu.SemaphoreType.DMA((2,)),
-        ],
-        out_specs=[vmem, vmem] + [anywhere] * len(passed),
-        input_output_aliases={3 + len(after) + i: 2 + i for i in range(len(passed))},
+    made = pl.pallas_call(
+        functools.partial(settle_kernel, len(groups), waits),
+        out_shape=outs + [jax.ShapeDtypeStruct(p.shape, p.dtype) for p in passed],
+        in_specs=[pl.BlockSpec(memory_space=pltpu.SMEM)] + [anywhere] * (len(ins) + waits),
+        scratch_shapes=[pltpu.VMEM(shape, jnp.bfloat16) for shape in shapes]
+        + [pltpu.SemaphoreType.DMA((len(ins),))],
+        out_specs=[vmem] * len(outs) + [anywhere] * len(passed),
+        input_output_aliases={1 + len(ins) + len(after) + i: len(outs) + i for i in range(len(passed))},
         compiler_params=pltpu.CompilerParams(vmem_limit_bytes=VM),
         cost_estimate=lasts(3),
         name="settle_%s" % label,
-    )(bit.reshape(1), keep.reshape(shape), got.reshape(shape), *after, *passed)
-    return stay.reshape(-1, rows, columns), go.reshape(-1, rows, columns), *passed
+    )(jnp.stack(bits), *ins, *after, *passed)
+    sides = [x.reshape((-1,) + x.shape[2:]) for x in made[: len(outs)]]
+    return list(zip(sides[::2], sides[1::2])), made[len(outs) :]
 
 
 def settle_mix_kernel(near_ref, got_ref, *refs):
@@ -1598,18 +1599,23 @@
     scalars = jnp.stack([first_local, lax.rem(dp_index, 2)])
     experts, chains = [], []
 
-    def advance(j, after, come=None, passed=()):
-        masks, stay, go = chains[j]
-        come = swap(go, "dp", masks[0]) if come is None else come
-        stay, go, *passed = settle(stay, come, masks[1], "%d_%d" % (j, masks[1]), after, passed)
-        chains[j] = (masks[1:], stay, go)
-        return (stay, *passed) if passed else stay
+    def advance(which, after, comes=(), passed=()):
+        comes = dict(comes)
+        groups = []
+        for j in which:
+            masks, stay, go = chains[j]
+            groups.append((stay, comes[j] if j in comes else swap(go, "dp", masks[0]), masks[1]))
+        label = "_".join("%d_%d" % (j, chains[j][0][1]) for j in which)
+        sides, passed = settle(groups, label, after, passed)
+        for j, (stay, go) in zip(which, sides):
+            chains[j] = (chains[j][0][1:], stay, go)
+        return [chains[j][1] for j in which], passed
 
     masks = [1] + [1 << b for b in range(2, dp_count.bit_length() - 1)] + [PAIR]
     for j in range(half_experts):
         after = [experts[-1][2]] if experts else []
         if j == 3:
-            after.append(advance(0, after))
+            after += advance([0], after)[0]
         experts.append(
             run_expert(
                 scalars, j, received, arrived, scale, gate_up_weight, down_weight, dp_count, after
@@ -1617,15 +1623,11 @@
         )
         chains.append((masks, experts[j][0], experts[j][1]))
     mine, theirs = combine(code, [e[2] for e in experts], capacity, [])
-    steps = [advance(1, [mine])]
+    steps, _ = advance([1], [mine])
     normed_f_grad, near_mix, far_mix, come = return_sums(
         code, mine, theirs, [e[3] for e in experts], capacity, chains[1][2], chains[1][0][0], 6, steps
     )
-    steps = [normed_f_grad]
-    steps.append(advance(0, steps))
-    stay, far_mix = advance(2, steps[-1:], None, [far_mix])
-    steps.append(stay)
-    steps.append(advance(1, steps[-1:], come))
+    steps, (far_mix,) = advance([2, 0, 1], [normed_f_grad], [(1, come)], [far_mix])
     input_grad, dense = attend_back(
         hidden_in, out_grad, middle, normed_f_grad, normed, qkv, attended, lse, ids, norm_gains, qkv_weight,
         out_weight, steps
@@ -1698,7 +1700,7 @@
         dense_own = reduce_dense_far(dense)
         for j in range(half_experts):
             while len(chains[j][0]) > 1:
-                advance(j, [dense_own])
+                advance([j], [dense_own])
         own_parts = [c[1][0] for c in chains]
         other_parts = [swap_pair(c[2][0]) for c in chains]
         own = jnp.stack(own_parts).astype(jnp.float32)

time: 377 us -> 376 us (level)
    pallas_call x5 -> x3, Pallas kernels: 14.7 us -> 11.8 us  [settle(): pl.pallas_call(functools.partial(settle_kernel, len(groups), waits), out_...]
  transfers between devices with their start and end apart: 11 -> 11, of which waited for: 1 -> 2; matrix products, arithmetic and copies ran while one was open for 0% -> 1% of each run, Pallas kernels for 47% -> 46%
where the time goes in v1:
time: 376 us; the launch traced here: 372 us
  Pallas kernels  333 us (89%)
  starting transfers between devices  16.6 us (4%)
  waiting for transfers between devices  10.8 us (3%)
  other arithmetic  5.54 us (1%)
  local copies, waits for them, and re-layouts  4.33 us (1%)
    pallas_call x1, Pallas kernels, finish(): pl.pallas_call(functools.partial(finish_kernel, count, groups, 4, orders,...  88.1 us
    pallas_call x4, Pallas kernels, run_expert(): pl.pallas_call(functools.partial(expert_kernel, j, owners, tiles, len(aft...  74.6 us
    pallas_call x1, Pallas kernels, return_sums(): pl.pallas_call(functools.partial(return_kernel, capacity, count, far_mask...  52.2 us
    pallas_call x1, Pallas kernels, gather_and_select(): pl.pallas_call(functools.partial(gather_kernel, capacity, experts_here, h...  44.6 us
    pallas_call x1, Pallas kernels, attend_back(): pl.pallas_call(functools.partial(attend_back_kernel, len(after)), out_sha...  22.9 us
    pallas_call x1, Pallas kernels, attend(): pl.pallas_call(attend_kernel, out_shape=(shape((rows, width), jnp.bfloat1...  17.8 us
    ppermute x11, starting transfers between devices, swap(): return lax.ppermute(values, axis, [(i, i ^ mask) for i in range(count)])  16.6 us
    pallas_call x3, Pallas kernels, settle(): pl.pallas_call(functools.partial(settle_kernel, len(groups), waits), out_...  11.8 us
  transfers between devices with their start and end apart: 11, of which 2 were waited for; matrix products, arithmetic and copies ran while one was open for 1% of the time, Pallas kernels for 46%

profile of v1, /device:TPU:0, one launch (start us, length us, event | category | flops | bytes accessed | tf_op | source)
XLA Modules:
  0.0 372.0 jit_solution(289373574799017650)
XLA Ops:
  2.2 1.5 convert_element_type.17
  3.8 3.1 collective-permute-start.1
  6.9 1.5 collective-permute-start
  9.1 17.8 %attend.1 = (bf16[384,1024]{1,0:T(8,128)(2,1)}, bf16[384,2048]{1,0:T(8,128)(2,1)}, bf16[384,1024]{1,0:T(8,128)(2,1)}, f32[384,128]{1,0:T(8,128)}, f32[384,1024]{1,0:T(8,128)}, /*index=5*/bf16[384,1024]{1,0:T(8,128)(2,1)}) custom-call(f32[384,1024]{1,0:T(8,128)} %hidden_hbm.1, s32[3,384]{1,0:T(4,128)} %pad_add_fusion.ids_ref, bf16[2,1024]{1,0:T(2,128)(2,1)} %gains_ref.3, ...), custom_call_target="tpu_custom_call" | custom-call | flops 18000000 | bytes 1024 | tf_op jit(solution)/shard_map/attend/pallas_call | solution.py:285
  28.6 44.6 %gather_and_select.1 = (bf16[4,8,144,1024]{3,2,1,0:T(8,128)(2,1)}, bf16[4,8,144,1024]{3,2,1,0:T(8,128)(2,1)}, f32[4,8,144,1]{3,2,1,0:T(8,128)}, f32[8,4,384]{2,1,0:T(4,128)}) custom-call(bf16[384,1024]{1,0:T(8,128)(2,1)} %get-tuple-element.87.token_ref, bf16[416,1024]{1,0:T(8,128)(2,1)} %copy-done.1, bf16[416,1024]{1,0:T(8,128)(2,1)} %copy-done.7, ...), custom_call_target="tpu_custom_call" | custom-call | flops 44000000 | bytes 1024 | tf_op jit(solution)/shard_map/gather_and_select/pallas_call | solution.py:730
  73.3 18.8 %expert_0.1 = (bf16[4,192,1024]{2,1,0:T(8,128)(2,1)}, bf16[4,192,1024]{2,1,0:T(8,128)(2,1)}, bf16[1152,1024]{1,0:T(8,128)(2,1)}, bf16[1152,1024]{1,0:T(8,128)(2,1)}) custom-call(s32[2]{0:T(128)} %pad_add_fusion.3.s_ref, bf16[4,8,144,1024]{3,2,1,0:T(8,128)(2,1)} %get-tuple-element.88.rec_hbm, bf16[4,8,144,1024]{3,2,1,0:T(8,128)(2,1)} %get-tuple-element.89.arr_hbm, ...), custom_call_target="tpu_custom_call" | custom-call | flops 18000000 | bytes 1024 | tf_op jit(solution)/shard_map/expert_0/pallas_call | solution.py:121
  92.1 1.6 collective-permute-start.3
  93.6 18.5 %expert_1.1 = (bf16[4,192,1024]{2,1,0:T(8,128)(2,1)}, bf16[4,192,1024]{2,1,0:T(8,128)(2,1)}, bf16[1152,1024]{1,0:T(8,128)(2,1)}, bf16[1152,1024]{1,0:T(8,128)(2,1)}) custom-call(s32[2]{0:T(128)} %pad_add_fusion.3.s_ref, bf16[4,8,144,1024]{3,2,1,0:T(8,128)(2,1)} %get-tuple-element.88.rec_hbm, bf16[4,8,144,1024]{3,2,1,0:T(8,128)(2,1)} %get-tuple-element.89.arr_hbm, ...), custom_call_target="tpu_custom_call" | custom-call | flops 18000000 | bytes 1024 | tf_op jit(solution)/shard_map/expert_1/pallas_call | solution.py:121
  112.8 18.9 %expert_2.1 = (bf16[4,192,1024]{2,1,0:T(8,128)(2,1)}, bf16[4,192,1024]{2,1,0:T(8,128)(2,1)}, bf16[1152,1024]{1,0:T(8,128)(2,1)}, bf16[1152,1024]{1,0:T(8,128)(2,1)}) custom-call(s32[2]{0:T(128)} %pad_add_fusion.3.s_ref, bf16[4,8,144,1024]{3,2,1,0:T(8,128)(2,1)} %get-tuple-element.88.rec_hbm, bf16[4,8,144,1024]{3,2,1,0:T(8,128)(2,1)} %get-tuple-element.89.arr_hbm, ...), custom_call_target="tpu_custom_call" | custom-call | flops 18000000 | bytes 1024 | tf_op jit(solution)/shard_map/expert_2/pallas_call | solution.py:121
  131.7 1.6 collective-permute-start.2
  133.2 3.3 settle_0_4.1
  136.6 2.6 collective-permute-start.4
  139.8 18.3 %expert_3.1 = (bf16[4,192,1024]{2,1,0:T(8,128)(2,1)}, bf16[4,192,1024]{2,1,0:T(8,128)(2,1)}, bf16[1152,1024]{1,0:T(8,128)(2,1)}, bf16[1152,1024]{1,0:T(8,128)(2,1)}) custom-call(s32[2]{0:T(128)} %pad_add_fusion.3.s_ref, bf16[4,8,144,1024]{3,2,1,0:T(8,128)(2,1)} %get-tuple-element.88.rec_hbm, bf16[4,8,144,1024]{3,2,1,0:T(8,128)(2,1)} %get-tuple-element.89.arr_hbm, ...), custom_call_target="tpu_custom_call" | custom-call | flops 18000000 | bytes 1024 | tf_op jit(solution)/shard_map/expert_3/pallas_call | solution.py:121
  159.0 10.6 %combine.1 = (bf16[4,384,1024]{2,1,0:T(8,128)(2,1)}, bf16[4,384,1024]{2,1,0:T(8,128)(2,1)}) custom-call(f32[8,4,384]{2,1,0:T(4,128)} %get-tuple-element.102.code_ref, bf16[1152,1024]{1,0:T(8,128)(2,1)} %get-tuple-element.91.refs_0_, bf16[1152,1024]{1,0:T(8,128)(2,1)} %get-tuple-element.92.refs_0_.refs_1_, ...), custom_call_target="tpu_custom_call" | custom-call | flops 12000000 | bytes 1024 | tf_op jit(solution)/shard_map/combine/pallas_call | solution.py:808
  169.5 3.3 settle_1_4.1
  172.9 52.2 %return_sums.1 = (f32[384,1024]{1,0:T(8,128)}, bf16[2,384,1024]{2,1,0:T(8,128)(2,1)}, bf16[2,384,1024]{2,1,0:T(8,128)(2,1)}, bf16[2,192,1024]{2,1,0:T(8,128)(2,1)}) custom-call(f32[8,4,384]{2,1,0:T(4,128)} %get-tuple-element.102.code_ref, bf16[4,384,1024]{2,1,0:T(8,128)(2,1)} %get-tuple-element.104.refs_2_.mine_ref, ...), custom_call_target="tpu_custom_call" | custom-call | flops 37000000 | bytes 1024 | tf_op jit(solution)/shard_map/return_sums/pallas_call | solution.py:888
  225.1 1.1 copy-done.5
  226.5 5.2 %settle_2_4_0_2_1_2.1 = (bf16[1,2,192,1024]{3,2,1,0:T(8,128)(2,1)}, bf16[1,2,192,1024]{3,2,1,0:T(8,128)(2,1)}, bf16[1,1,192,1024]{3,2,1,0:T(8,128)(2,1)}, bf16[1...) custom-call(s32[3]{0:T(128)} %pad_add_fusion.2.bits_ref, ...), custom_call_target="tpu_custom_call", output_to_operand_aliasing={{6}: (8, {})} | custom-call | flops 3000000 | bytes 1024 | tf_op jit(solution)/shard_map/settle_2_4_0_2_1_2/pallas_call | solution.py:946
  231.6 1.8 collective-permute-start.10
  233.7 2.7 collective-permute-start.7
  237.1 22.9 %attend_back.1 = (f32[384,1024]{1,0:T(8,128)}, bf16[1024,3200]{1,0:T(8,128)(2,1)}) custom-call(f32[384,1024]{1,0:T(8,128)} %grad_ref.1, f32[384,1024]{1,0:T(8,128)} %get-tuple-element.119.middle_ref.refs_15_, f32[384,1024]{1,0:T(8,128)} %get-tuple-element.113.refs_6_.normed_grad_ref, f32[384,128]{1,0:T(8,128)} %get-tuple-element.120.lse_ref, ...), custom_call_target="tpu_custom_call" | custom-call | flops 26000000 | bytes 1024 | tf_op jit(solution)/shard_map/attend_back/pallas_call | solution.py:434
  260.4 10.4 %collective-permute-done.6.refs_3_.refs_2_ = bf16[192,1024]{1,0:T(8,128)(2,1)S(1)} collective-permute-done((bf16[192,1024]{1,0:T(8,128)(2,1)}, bf16[192,1024]{1,0:T(8,128)(2,1)S(1)}, u32[]{:S(2)}, u32[]{:S(2)}) %collective-permute-start.6) | collective-permute-done | bytes 393248 | tf_op jit(solution)/shard_map/ppermute | solution.py:1485
  272.6 88.1 %finish.1 = (bf16[2,2,32,3200]{3,2,1,0:T(8,128)(2,1)}, bf16[4,192,1024]{2,1,0:T(8,128)(2,1)}, bf16[384,1024]{1,0:T(8,128)(2,1)}, f32[8,8,512]{2,1,0:T(8,128)}, f...) custom-call(bf16[2,2,2,2,2,32,3200]{6,5,4,3,2,1,0:T(8,128)(2,1)} %bi, ...), custom_call_target="tpu_custom_call" | custom-call | flops 75000000 | bytes 1024 | tf_op jit(solution)/shard_map/finish/pallas_call | solution.py:1278
  360.6 11.0 %update.1 = (f32[384,1024]{1,0:T(8,128)}, f32[8,128,1024]{2,1,0:T(8,128)}, f32[8,64,1024]{2,1,0:T(8,128)}, f32[8,128]{1,0:T(8,128)}, f32[8,64]{1,0:T(8,128)}, /*...) custom-call(s32[2]{0:T(128)} %pad_add_fusion.1.s_ref, ...), custom_call_target="tpu_custom_call" | custom-call | flops 6000000 | bytes 1024 | tf_op jit(solution)/shard_map/update/pallas_call | solution.py:1453
  (48 shorter events, 9.4 us)
Async XLA Ops:
  2.2 6.3 %copy-start.9 = (s32[384]{0:T(512)S(1)}, s32[384]{0:T(512)}, u32[]{:S(2)}) copy-start(s32[384]{0:T(512)} %param.23) | copy-start | bytes 4612
  2.2 6.3 %copy-start.10 = (s32[384]{0:T(512)S(1)}, s32[384]{0:T(512)}, u32[]{:S(2)}) copy-start(s32[384]{0:T(512)} %param.24) | copy-start | bytes 4612
  2.2 6.3 %copy-start.11 = (s32[384]{0:T(512)S(1)}, s32[384]{0:T(512)}, u32[]{:S(2)}) copy-start(s32[384]{0:T(512)} %param.25) | copy-start | bytes 4612
  3.8 23.1 %copy-start.1 = (bf16[416,1024]{1,0:T(8,128)(2,1)}, bf16[416,1024]{1,0:T(8,128)(2,1)S(1)}, u32[]{:S(2)}) copy-start(bf16[416,1024]{1,0:T(8,128)(2,1)S(1)} %fusion.1.grad_ref) | copy-start | bytes 2555908
  3.8 23.6 %collective-permute-start.1 = (bf16[416,1024]{1,0:T(8,128)(2,1)S(1)}, bf16[416,1024]{1,0:T(8,128)(2,1)S(1)}, u32[]{:S(2)}, u32[]{:S(2)}) collective-permute-start(bf16[416,1024]{1,0:T(8,128)(2,1)S(1)} %fusion.1.grad_ref), channel_id=1, source_target_pairs={{0,8},{4,12},{8,0},{12,4},{16,24},{20,28},{24,16},{28,20},{1,9},{5... | collective-permute-start | bytes 2555912 | tf_op jit(solution)/shard_map/ppermute | solution.py:1485
  6.9 20.6 %collective-permute-start = (bf16[416,1024]{1,0:T(8,128)(2,1)S(1)}, bf16[416,1024]{1,0:T(8,128)(2,1)S(1)}, u32[]{:S(2)}, u32[]{:S(2)}) collective-permute-start(bf16[416,1024]{1,0:T(8,128)(2,1)S(1)} %fusion.1.grad_ref), channel_id=1, source_target_pairs={{0,2},{1,3},{2,0},{3,1},{4,6},{5,7},{6,4},{7,5},{8,10},{9,11},{10,... | collective-permute-start | bytes 2555912 | tf_op jit(solution)/shard_map/ppermute | solution.py:1485
  27.5 0.9 copy-start.6
  27.5 1.2 copy-start.7
  92.1 41.2 %collective-permute-start.3 = (bf16[4,192,1024]{2,1,0:T(8,128)(2,1)}, bf16[4,192,1024]{2,1,0:T(8,128)(2,1)}, u32[]{:S(2)}, u32[]{:S(2)}) collective-permute-start(bf16[4,192,1024]{2,1,0:T(8,128)(2,1)} %get-tuple-element.96), channel_id=1, source_target_pairs={{0,4},{4,0},{8,12},{12,8},{16,20},{20,16},{24,28},{28,24},{1,5},{5... | collective-permute-start | bytes 4718600 | tf_op jit(solution)/shard_map/ppermute | solution.py:1485
  112.2 57.4 %collective-permute-start.5 = (bf16[4,192,1024]{2,1,0:T(8,128)(2,1)}, bf16[4,192,1024]{2,1,0:T(8,128)(2,1)}, u32[]{:S(2)}, u32[]{:S(2)}) collective-permute-start(bf16[4,192,1024]{2,1,0:T(8,128)(2,1)} %get-tuple-element.101), channel_id=1, source_target_pairs={{0,4},{4,0},{8,12},{12,8},{16,20},{20,16},{24,28},{28,24},{1,5},{5... | collective-permute-start | bytes 4718600 | tf_op jit(solution)/shard_map/ppermute | solution.py:1485
  131.7 93.4 %collective-permute-start.2 = (bf16[4,192,1024]{2,1,0:T(8,128)(2,1)}, bf16[4,192,1024]{2,1,0:T(8,128)(2,1)S(1)}, u32[]{:S(2)}, u32[]{:S(2)}) collective-permute-start(bf16[4,192,1024]{2,1,0:T(8,128)(2,1)} %get-tuple-element.94), channel_id=1, source_target_pairs={{0,4},{4,0},{8,12},{12,8},{16,20},{20,16},{24,28},{28,24},{1,5},{5... | collective-permute-start | bytes 4718600 | tf_op jit(solution)/shard_map/ppermute | solution.py:1485
  136.6 88.5 %collective-permute-start.4 = (bf16[2,192,1024]{2,1,0:T(8,128)(2,1)}, bf16[2,192,1024]{2,1,0:T(8,128)(2,1)S(1)}, u32[]{:S(2)}, u32[]{:S(2)}) collective-permute-start(bf16[2,192,1024]{2,1,0:T(8,128)(2,1)} %bitcast.70), channel_id=1, source_target_pairs={{0,16},{4,20},{8,24},{12,28},{16,0},{20,4},{24,8},{28,12},{1,17},{... | collective-permute-start | bytes 2359304 | tf_op jit(solution)/shard_map/ppermute | solution.py:1485
  158.2 112.6 %collective-permute-start.9 = (bf16[4,192,1024]{2,1,0:T(8,128)(2,1)}, bf16[4,192,1024]{2,1,0:T(8,128)(2,1)S(1)}, u32[]{:S(2)}, u32[]{:S(2)}) collective-permute-start(bf16[4,192,1024]{2,1,0:T(8,128)(2,1)} %get-tuple-element.128), channel_id=1, source_target_pairs={{0,4},{4,0},{8,12},{12,8},{16,20},{20,16},{24,28},{28,24},{1,5},{5... | collective-permute-start | bytes 4718600 | tf_op jit(solution)/shard_map/ppermute | solution.py:1485
  225.1 1.1 copy-start.5
  225.1 1.4 copy-start.8
  231.6 39.2 %collective-permute-start.10 = (bf16[2,384,1024]{2,1,0:T(8,128)(2,1)}, bf16[2,384,1024]{2,1,0:T(8,128)(2,1)S(1)}, u32[]{:S(2)}, u32[]{:S(2)}) collective-permute-start(bf16[2,384,1024]{2,1,0:T(8,128)(2,1)} %get-tuple-element.130), channel_id=1, source_target_pairs={{0,2},{1,3},{2,0},{3,1},{4,6},{5,7},{6,4},{7,5},{8,10},{9,11},{10,... | collective-permute-start | bytes 4718600 | tf_op jit(solution)/shard_map/ppermute | solution.py:1485
  233.5 37.3 %collective-permute-start.8 = (bf16[2,192,1024]{2,1,0:T(8,128)(2,1)}, bf16[2,192,1024]{2,1,0:T(8,128)(2,1)}, u32[]{:S(2)}, u32[]{:S(2)}) collective-permute-start(bf16[2,192,1024]{2,1,0:T(8,128)(2,1)} %bitcast.71), channel_id=1, source_target_pairs={{0,16},{4,20},{8,24},{12,28},{16,0},{20,4},{24,8},{28,12},{1,17},{... | collective-permute-start | bytes 2359304 | tf_op jit(solution)/shard_map/ppermute | solution.py:1485
  233.7 26.7 %collective-permute-start.7 = (bf16[192,1024]{1,0:T(8,128)(2,1)}, bf16[192,1024]{1,0:T(8,128)(2,1)S(1)}, u32[]{:S(2)}, u32[]{:S(2)}) collective-permute-start(bf16[192,1024]{1,0:T(8,128)(2,1)} %bitcast.73), channel_id=1, source_target_pairs={{0,8},{4,12},{8,0},{12,4},{16,24},{20,28},{24,16},{28,20},{1,9},{5... | collective-permute-start | bytes 1179656 | tf_op jit(solution)/shard_map/ppermute | solution.py:1485
  236.4 34.4 %collective-permute-start.6 = (bf16[192,1024]{1,0:T(8,128)(2,1)}, bf16[192,1024]{1,0:T(8,128)(2,1)S(1)}, u32[]{:S(2)}, u32[]{:S(2)}) collective-permute-start(bf16[192,1024]{1,0:T(8,128)(2,1)} %bitcast.72), channel_id=1, source_target_pairs={{0,8},{4,12},{8,0},{12,4},{16,24},{20,28},{24,16},{28,20},{1,9},{5... | collective-permute-start | bytes 1179656 | tf_op jit(solution)/shard_map/ppermute | solution.py:1485
  260.4 10.4 %copy-start.2 = (bf16[192,1024]{1,0:T(8,128)(2,1)}, bf16[192,1024]{1,0:T(8,128)(2,1)S(1)}, u32[]{:S(2)}) copy-start(bf16[192,1024]{1,0:T(8,128)(2,1)S(1)} %collective-permute-done.7.refs_4_.refs_3_) | copy-start | bytes 1179652
  270.8 0.8 copy-start.3
  270.8 1.3 copy-start.4
  270.8 1.8 copy-start
